TPU v7x, 512 devices: a whole 4x4x16 slice. The times are simulated.
512 devices in a mesh: ctx: 64 (over y_hi, z, core), head: 8 (over y_lo, x).
Axes of the slice: x: 4, y: 4 (y_hi: 2, y_lo: 2; y = y_hi * 2 + y_lo), z: 16, core: 2. Of those that a mesh axis runs over, the one named last changes fastest.
Arguments:
- queries: bfloat16 [512, 8192], P(('ctx', 'head')), may hold values from -120 to 120
- out_grad: bfloat16 [512, 8192], P(('ctx', 'head')), may hold values from -6 to 6
- resp_keys: bfloat16 [512, 1024], P('ctx', 'head'), may hold values from -6 to 6
- resp_values: bfloat16 [512, 1024], P('ctx', 'head'), may hold values from -6 to 6
- prompt_keys: bfloat16 [49152, 1024], P('ctx', 'head'), may hold values from -6 to 6
- prompt_values: bfloat16 [49152, 1024], P('ctx', 'head'), may hold values from -6 to 6
- resp_lengths: int32 [16], replicated, may hold values from 1 to 32, 256 in all
- resp_order: int32 [16], replicated, may hold values from 0 to 15, each once
Outputs:
- query_grad: bfloat16 [512, 8192], P(('ctx', 'head'))
- prompt_key_grad: bfloat16 [49152, 1024], P('ctx', 'head')
- prompt_value_grad: bfloat16 [49152, 1024], P('ctx', 'head')
- resp_key_grad: bfloat16 [512, 1024], P('ctx', 'head')
- resp_value_grad: bfloat16 [512, 1024], P('ctx', 'head')
Inputs may be any that keep to these rules, and one draw needn't show every extreme that they name: `resp_lengths`: each response has 1 to 32 tokens, 256 in all, and one has exactly 32. `resp_order`: each response stands in exactly one slot.
All inputs are finite; a program needn't handle non-finite values.
Results may differ from a plain program's by a relative error of at most 0.017.
Values may be sent and summed in bfloat16 or wider, within the bound.
No kernel may reach another device: no remote copies, remote signals or barrier semaphores. Data moves between devices by JAX's collectives and lax.ppermute only.
A program may use at most 64 MiB of HBM per device.

v0:
```python
import math

import jax
import jax.numpy as jnp
from jax import lax
from jax.sharding import PartitionSpec as P

QH = 64
KVH = 8
HD = 128
NRESP = 16


def shards(
    queries, out_grad, resp_keys, resp_values, prompt_keys, prompt_values, resp_lengths, resp_order
):
    n_ctx = lax.axis_size("ctx")
    me_ctx = lax.axis_index("ctx")
    rows_dev = resp_keys.shape[0]
    prompt_rows = prompt_keys.shape[0]
    kv_dev = resp_keys.shape[1] // HD
    group = QH // KVH
    total_rows = rows_dev * n_ctx
    slot_rows = total_rows // NRESP
    scale = 1.0 / math.sqrt(HD)
    local_q, local_grad = (
        lax.all_to_all(queries, "head", split_axis=1, concat_axis=0, tiled=True),
        lax.all_to_all(out_grad, "head", split_axis=1, concat_axis=0, tiled=True),
    )
    all_q, all_grad = (
        lax.all_gather(local_q, "ctx", axis=0, tiled=True),
        lax.all_gather(local_grad, "ctx", axis=0, tiled=True),
    )
    rows = jnp.arange(total_rows, dtype=jnp.int32)
    slot = rows // slot_rows
    offset = rows % slot_rows
    slot_ids = jnp.arange(NRESP, dtype=jnp.int32)
    slot_len = jnp.sum(
        jnp.where(resp_order[:, None] == slot_ids[None, :], resp_lengths[None, :], 0), axis=1
    )
    row_len = jnp.sum(jnp.where(slot[:, None] == slot_ids[None, :], slot_len[None, :], 0), axis=1)
    live = offset < row_len
    key_rows = me_ctx * rows_dev + jnp.arange(rows_dev, dtype=jnp.int32)
    key_slot = key_rows // slot_rows
    key_offset = key_rows % slot_rows
    keys = jnp.concatenate([prompt_keys, resp_keys], axis=0).reshape(-1, kv_dev, HD)
    values = jnp.concatenate([prompt_values, resp_values], axis=0).reshape(-1, kv_dev, HD)
    grad_set = jnp.where(live[:, None], all_grad, jnp.zeros_like(all_grad))
    count = all_q.shape[0]
    block = math.gcd(count, max(8, 512 // group))
    blocks = count // block
    q_blocks = all_q.reshape(blocks, block, kv_dev, group, HD)
    g_blocks = grad_set.reshape(blocks, block, kv_dev, group, HD)
    s_blocks = slot.reshape(blocks, block)
    o_blocks = offset.reshape(blocks, block)

    def logits_of(q_blk, slot_blk, off_blk):
        raw = jnp.einsum("rjgd,kjd->jrgk", q_blk, keys, preferred_element_type=jnp.float32) * scale
        own = (slot_blk[:, None] == key_slot[None, :]) & (key_offset[None, :] <= off_blk[:, None])
        visible = jnp.concatenate([jnp.ones((block, prompt_rows), bool), own], axis=1)
        return jnp.where(visible[None, :, None, :], raw, -1e30)

    def first_pass(inputs):
        q_blk, g_blk, slot_blk, off_blk = inputs
        logits = logits_of(q_blk, slot_blk, off_blk)
        top = jnp.max(logits, axis=-1)
        weights = jnp.exp(logits - top[..., None])
        dprob = jnp.einsum("rjgd,kjd->jrgk", g_blk, values, preferred_element_type=jnp.float32)
        return (top, jnp.sum(weights, axis=-1), jnp.sum(weights * dprob, axis=-1))

    tops, totals, inners = lax.map(first_pass, (q_blocks, g_blocks, s_blocks, o_blocks))
    top = lax.pmax(tops, "ctx")
    factor = jnp.exp(tops - top)
    total, inner = lax.psum((totals * factor, inners * factor), "ctx")
    delta = inner / total

    def second_pass(carry, inputs):
        key_grad, value_grad = carry
        q_blk, g_blk, slot_blk, off_blk, top_blk, total_blk, delta_blk = inputs
        logits = logits_of(q_blk, slot_blk, off_blk)
        prob = jnp.exp(logits - top_blk[..., None]) / total_blk[..., None]
        dprob = jnp.einsum("rjgd,kjd->jrgk", g_blk, values, preferred_element_type=jnp.float32)
        dscore = (prob * (dprob - delta_blk[..., None])).astype(jnp.bfloat16)
        prob_low = prob.astype(jnp.bfloat16)
        q_grad = (
            jnp.einsum("jrgk,kjd->rjgd", dscore, keys, preferred_element_type=jnp.float32) * scale
        )
        key_grad = (
            key_grad
            + jnp.einsum("jrgk,rjgd->kjd", dscore, q_blk, preferred_element_type=jnp.float32)
            * scale
        )
        value_grad = value_grad + jnp.einsum(
            "jrgk,rjgd->kjd", prob_low, g_blk, preferred_element_type=jnp.float32
        )
        return ((key_grad, value_grad), q_grad)

    start = jnp.zeros((prompt_rows + rows_dev, kv_dev, HD), jnp.float32)
    (key_grad, value_grad), q_grads = lax.scan(
        second_pass, (start, start), (q_blocks, g_blocks, s_blocks, o_blocks, top, total, delta)
    )
    q_terms = q_grads.reshape(count, kv_dev * group * HD)
    mine = lax.psum_scatter(q_terms, "ctx", scatter_dimension=0, tiled=True).astype(jnp.bfloat16)
    query_grad = lax.all_to_all(mine, "head", split_axis=0, concat_axis=1, tiled=True)
    key_flat = key_grad.reshape(prompt_rows + rows_dev, kv_dev * HD).astype(jnp.bfloat16)
    value_flat = value_grad.reshape(prompt_rows + rows_dev, kv_dev * HD).astype(jnp.bfloat16)
    return (
        query_grad,
        key_flat[:prompt_rows],
        value_flat[:prompt_rows],
        key_flat[prompt_rows:],
        value_flat[prompt_rows:],
    )


def solution(mesh):
    in_specs = (
        P(("ctx", "head"), None),
        P(("ctx", "head"), None),
        P("ctx", "head"),
        P("ctx", "head"),
        P("ctx", "head"),
        P("ctx", "head"),
        P(),
        P(),
    )
    out_specs = (
        P(("ctx", "head"), None),
        P("ctx", "head"),
        P("ctx", "head"),
        P("ctx", "head"),
        P("ctx", "head"),
    )
    return jax.shard_map(shards, mesh=mesh, in_specs=in_specs, out_specs=out_specs, check_vma=False)
```

profile of v0, /device:TPU:24, one launch (start us, length us, event | category | flops | bytes accessed | tf_op | source)
XLA Modules:
  0.0 1170.8 jit_solution(15957239229014960005)
XLA Ops:
  7.8 1.5 reduce.6
  9.3 10.3 all_to_all.48
  20.3 1.5 reduce.7
  21.8 8.6 all_to_all.49
  32.7 1.1 maximum_bitcast_fusion
  33.8 127.8 %all-gather.5.cloned.1.call-done = bf16[1,512,1024]{2,1,0:T(8,128)(2,1)} async-done(((bf16[1,8,1024]{2,1,0:T(8,128)(2,1)}), bf16[1,512,1024]{2,1,0:T(8,128)(2,1)}) %all-gather.5.cloned.1.call-update) | async-done | bytes 1048592 | tf_op jit(solution)/shard_map/all_gather | solution.py:31
  161.6 1.5 copy.60
  163.1 137.7 %all-gather.7.cloned.1.call-done = bf16[1,512,1024]{2,1,0:T(8,128)(2,1)} async-done(((bf16[1,8,1024]{2,1,0:T(8,128)(2,1)}), bf16[1,512,1024]{2,1,0:T(8,128)(2,1)}) %all-gather.7.cloned.1.call-update) | async-done | bytes 1048592 | tf_op jit(solution)/shard_map/all_gather | solution.py:32
  300.8 1.4 fusion.45
  302.5 55.1 %while.33 = (s32[]{:T(128)}, f32[8,1,64,8]{3,2,1,0:T(8,128)S(1)}, f32[8,1,64,8]{3,2,1,0:T(8,128)}, f32[8,1,64,8]{3,2,1,0:T(8,128)}, s32[8,64]{1,0:T(8,128)}, /*i...) while((s32[]{:T(128)}, f32[8,1,64,8]{3,2,1,0:T(8,128)S(1)}, ...), condition=%wide.region_6.7_spmd.clone.clone, body=%wide.region_2.6_spmd.clone.clone.sunk | while | flops 208191712 | bytes 6066982 | solution.py:71
  304.5 1.4 copy.68
  311.4 1.4 copy.68
  318.3 1.4 copy.68
  325.2 1.4 copy.68
  332.1 1.4 copy.68
  339.0 1.4 copy.68
  345.9 1.4 copy.68
  352.7 1.4 copy.68
  358.3 259.3 %pmax.7 = f32[8,1,64,8]{3,2,1,0:T(8,128)S(1)} all-reduce(f32[8,1,64,8]{3,2,1,0:T(8,128)} %copy-done), channel_id=1, replica_groups=mesh['ctx'=64,'head'=8] {'ctx'}, use_global_device_ids=true, to_apply=%region_7.8 | all-reduce | flops 4096 | bytes 32768 | tf_op jit(solution)/shard_map/pmax | solution.py:72
  617.6 2.0 fusion.46
  619.6 259.6 %all-reduce.2 = (f32[8,1,64,8]{3,2,1,0:T(8,128)}, f32[8,1,64,8]{3,2,1,0:T(8,128)}) all-reduce(f32[8,1,64,8]{3,2,1,0:T(8,128)} %get-tuple-element.530, f32[8,1,64,8]{3,2,1,0:T(8,128)} %get-tuple-element.529), channel_id=1, replica_groups=mesh['ctx'=64,'head'=8] {'ctx'}, use_global_device_ids=true, to_apply=%region_8.9 | all-reduce | flops 8192 | bytes 65536 | tf_op jit(solution)/shard_map/psum | solution.py:74
  879.1 1.8 div.58
  880.9 62.8 %while.34 = (s32[]{:T(128)}, f32[776,1,128]{2,0,1:T(8,128)S(1)}, f32[776,1,128]{2,0,1:T(8,128)S(1)}, f32[8,64,1,8,128]{4,3,1,2,0:T(8,128)}, bf16[8,64,1,8,128]{4...) while((s32[]{:T(128)}, f32[776,1,128]{2,0,1:T(8,128)S(1)}, ...), condition=%wide.region_11.12_spmd.clone.clone.clone, body=%wide.region_10.11_spmd.clone.clone.clone.sunk | while | flops 512301728 | bytes 10959189 | solution.py:99
  882.3 1.4 copy.69
  885.1 0.9 exponential_divide_fusion.2
  887.6 1.1 fusion.98
  890.1 1.4 copy.69
  895.5 1.1 fusion.98
  897.9 1.4 copy.69
  900.8 0.9 exponential_divide_fusion.2
  903.3 1.1 fusion.98
  905.8 1.4 copy.69
  908.7 0.9 exponential_divide_fusion.2
  911.2 1.1 fusion.98
  913.6 1.4 copy.69
  919.0 1.1 fusion.98
  921.5 1.4 copy.69
  924.4 0.9 exponential_divide_fusion.2
  926.9 1.1 fusion.98
  929.3 1.4 copy.69
  932.2 0.9 exponential_divide_fusion.2
  934.7 1.1 fusion.98
  937.2 1.4 copy.69
  942.6 1.1 fusion.98
  943.7 3.4 copy.64
  949.1 202.1 %reduce-scatter.2.cloned.1.call-done = f32[8,1024]{1,0:T(8,128)} async-done(((f32[512,1024]{1,0:T(8,128)}), f32[8,1024]{1,0:T(8,128)}) %reduce-scatter.2.cloned.1.call-update) | async-done | bytes 32784 | tf_op jit(solution)/shard_map/reduce_scatter | solution.py:103
  1153.2 5.7 all-to-all-start.2
  1159.5 4.2 all-to-all-done.2
  (200 shorter events, 92.0 us)
Async XLA Ops:
  7.2 154.5 %all-gather.5.cloned.1.call-start = ((), (), s32[]{:S(2)}) async-start(), calls=%async_computation.5 | async-start | bytes 1064960 | tf_op jit(solution)/shard_map/all_gather | solution.py:31
  20.3 280.6 %all-gather.7.cloned.1.call-start = ((), (), s32[]{:S(2)}) async-start(), calls=%async_computation.6 | async-start | bytes 1064960 | tf_op jit(solution)/shard_map/all_gather | solution.py:32
  31.0 1120.1 %reduce-scatter.2.cloned.1.call-start = ((), (), s32[]{:S(2)}) async-start(), calls=%async_computation.4 | async-start | bytes 2129920 | tf_op jit(solution)/shard_map/reduce_scatter | solution.py:103
  357.6 0.7 copy-start
  1153.2 10.4 all-to-all-start.2
Sparse Core Ops, SparseCore 0:
  20.4 141.2 all-gather.4
  165.5 135.2 all-gather.6
  947.2 203.9 reduce-scatter.1
where the time goes:
time: 1170 us
  blocking collectives  538 us (46%)
  waiting for transfers between devices  472 us (40%)
  local copies, waits for them, and re-layouts  72.6 us (6%)
  matrix products  40.6 us (3%)
  other arithmetic  27.8 us (2%)
  between operations  13.9 us (1%)
    psum x1, blocking collectives, shards(): total, inner = lax.psum((totals * factor, inners * factor), 'ctx')  260 us
    pmax x1, blocking collectives, shards(): top = lax.pmax(tops, 'ctx')  259 us
    reduce_scatter x1, waiting for transfers between devices, shards(): lax.psum_scatter(q_terms, 'ctx', scatter_dimension=0, tiled=True)  202 us
    all_gather x1, waiting for transfers between devices, shards(): lax.all_gather(local_grad, 'ctx', axis=0, tiled=True)  138 us
    all_gather x1, waiting for transfers between devices, shards(): lax.all_gather(local_q, 'ctx', axis=0, tiled=True)  128 us
  transfers between devices with their start and end apart: 4, of which 4 were waited for; matrix products, arithmetic and copies ran while one was open for 1% of the time, Pallas kernels for 0%

commit v1 on v0

v1 whole, which is shorter than its diff:
```python
import functools
import math

import jax
import jax.numpy as jnp
from jax import lax
from jax.experimental import pallas as pl
from jax.experimental.pallas import tpu as pltpu
from jax.sharding import Mesh
from jax.sharding import PartitionSpec as P

QH = 64
KVH = 8
HD = 128
NRESP = 16
GROUP = QH // KVH
SLOT = 32
NZ = 16
ROWS = 8
BLOCK = ROWS * GROUP
CLASS = NZ * BLOCK
CHUNK = 256
CHUNKS = CLASS // CHUNK
PROMPT_DEV = 768
SHARDS = 4
KEYS = 384
SCALE = 1.0 / math.sqrt(HD)
SCALE2 = SCALE * math.log2(math.e)
F32 = jnp.float32
BF16 = jnp.bfloat16


def nt(a, b):
    return lax.dot_general(a, b, (((1,), (1,)), ((), ())), preferred_element_type=F32)


def nn(a, b):
    return jnp.dot(a, b, preferred_element_type=F32)


def live_rows(lengths_ref, order_ref, z):
    yh, c = lax.axis_index("yh"), lax.axis_index("c")
    length = lengths_ref[order_ref[yh * (NRESP // 2) + z // 2]]
    return jnp.clip(length - ((z % 2) * 2 + c) * ROWS, 0, ROWS)


def key_code():
    z = lax.axis_index("z")
    return (z // 2) * SLOT + (z % 2) * 2 * ROWS + lax.broadcasted_iota(jnp.int32, (2 * ROWS, 1), 0)


def row_code(info):
    first = (lax.broadcasted_iota(jnp.int32, (16, HD), 1) == 0).astype(BF16)
    return nt(first, info)[:1].astype(jnp.int32)


def seen_of(info):
    keys, rows = key_code(), row_code(info)
    return (rows >= keys) & (rows // SLOT == keys // SLOT)


def first_kernel(lengths_ref, order_ref, rows_ref, kv_ref, resp_ref, q_ref, g_ref, info_ref, stat_ref):
    q_ref[...] = jnp.zeros_like(q_ref)
    g_ref[...] = jnp.zeros_like(g_ref)
    info_ref[...] = jnp.zeros_like(info_ref)
    c = lax.axis_index("c")
    in_block = lax.broadcasted_iota(jnp.int32, (BLOCK, HD), 0)

    def pack(z, at):
        live = live_rows(lengths_ref, order_ref, z)
        place = pl.ds(pl.multiple_of(at * 16, 16), BLOCK)
        q_ref[place] = rows_ref[z, 0]
        g_ref[place] = jnp.where(in_block < live * GROUP, rows_ref[z, 1], jnp.zeros((), BF16))
        code = (z // 2) * SLOT + ((z % 2) * 2 + c) * ROWS + in_block // GROUP
        info_ref[place] = code.astype(F32).astype(BF16)
        return at + (live + 1) // 2

    pairs = lax.fori_loop(0, NZ, pack, 0)
    chunks = (pairs * 16 + CHUNK - 1) // CHUNK
    stat_ref[...] = jnp.zeros_like(stat_ref)

    def chunk(i, _):
        place = pl.ds(pl.multiple_of(i * CHUNK, CHUNK), CHUNK)
        q, g = q_ref[place], g_ref[place]
        seen = seen_of(info_ref[place])
        raw = nt(resp_ref[0], q)
        logits = jnp.where(seen, raw * SCALE2, -1e30)
        top = jnp.max(logits, axis=0, keepdims=True)
        top = jnp.maximum(top, -1e29)
        weights = jnp.exp2(logits - top)
        total = jnp.sum(weights, axis=0, keepdims=True)
        inner = jnp.sum(weights * nt(resp_ref[1], g), axis=0, keepdims=True)
        for s in range(SHARDS):
            for b in range(PROMPT_DEV // KEYS):
                logits = nt(kv_ref[s, b * KEYS : (b + 1) * KEYS], q) * SCALE2
                dprob = nt(kv_ref[s, PROMPT_DEV + b * KEYS : PROMPT_DEV + (b + 1) * KEYS], g)
                now = jnp.maximum(top, jnp.max(logits, axis=0, keepdims=True))
                weights = jnp.exp2(logits - now)
                factor = jnp.exp2(top - now)
                total = total * factor + jnp.sum(weights, axis=0, keepdims=True)
                inner = inner * factor + jnp.sum(weights * dprob, axis=0, keepdims=True)
                top = now
        stat_ref[pl.ds(i, 1)] = top + jnp.log2(total)
        stat_ref[pl.ds(CHUNKS + i, 1)] = inner / total
        return 0

    lax.fori_loop(0, chunks, chunk, 0)


def second_kernel(
    lengths_ref,
    order_ref,
    stats_ref,
    q_ref,
    g_ref,
    info_ref,
    kv_ref,
    resp_ref,
    qg_ref,
    kvg_ref,
    rg_ref,
    mix_ref,
    keyt_ref,
    kacc_ref,
    vacc_ref,
    racc_ref,
    qacc_ref,
):
    logs = stats_ref[:, :CHUNKS]
    top = jnp.max(logs, axis=0)
    weights = jnp.exp2(logs - top[None])
    total = jnp.sum(weights, axis=0)
    mix_ref[:CHUNKS] = top + jnp.log2(total)
    mix_ref[CHUNKS:] = jnp.sum(weights * stats_ref[:, CHUNKS:], axis=0) / total
    for s in range(SHARDS):
        keyt_ref[s] = kv_ref[s, :PROMPT_DEV].T
    kacc_ref[...] = jnp.zeros_like(kacc_ref)
    vacc_ref[...] = jnp.zeros_like(vacc_ref)
    racc_ref[...] = jnp.zeros_like(racc_ref)
    pairs = lax.fori_loop(
        0, NZ, lambda z, at: at + (live_rows(lengths_ref, order_ref, z) + 1) // 2, 0
    )
    chunks = (pairs * 16 + CHUNK - 1) // CHUNK

    def chunk(i, _):
        place = pl.ds(pl.multiple_of(i * CHUNK, CHUNK), CHUNK)
        q, g = q_ref[place], g_ref[place]
        log, delta = mix_ref[pl.ds(i, 1)], mix_ref[pl.ds(CHUNKS + i, 1)]
        seen = seen_of(info_ref[place])
        prob = jnp.where(seen, jnp.exp2(jnp.where(seen, nt(resp_ref[0], q) * SCALE2 - log, 0.0)), 0.0)
        dscore = (prob * (nt(resp_ref[1], g) - delta)).astype(BF16)
        racc_ref[0] += nn(dscore, q)
        racc_ref[1] += nn(prob.astype(BF16), g)
        qgrad = lax.dot_general(
            resp_ref[0], dscore, (((0,), (0,)), ((), ())), preferred_element_type=F32
        )
        for s in range(SHARDS):
            for b in range(PROMPT_DEV // KEYS):
                at = slice(b * KEYS, (b + 1) * KEYS)
                logits = nt(kv_ref[s, at], q) * SCALE2
                dprob = nt(kv_ref[s, PROMPT_DEV + b * KEYS : PROMPT_DEV + (b + 1) * KEYS], g)
                prob = jnp.exp2(logits - log)
                dscore = (prob * (dprob - delta)).astype(BF16)
                kacc_ref[s, at] += nn(dscore, q)
                vacc_ref[s, at] += nn(prob.astype(BF16), g)
                qgrad = qgrad + nn(keyt_ref[s, :, at], dscore)
        qacc_ref[place] = (qgrad * SCALE).T
        return 0

    lax.fori_loop(0, chunks, chunk, 0)
    in_block = lax.broadcasted_iota(jnp.int32, (BLOCK, HD), 0)

    def unpack(z, at):
        live = live_rows(lengths_ref, order_ref, z)
        block = qacc_ref[pl.ds(pl.multiple_of(at * 16, 16), BLOCK)]
        qg_ref[pl.ds(pl.multiple_of(z * BLOCK, BLOCK), BLOCK)] = jnp.where(
            in_block < live * GROUP, block, 0.0
        ).astype(BF16)
        return at + (live + 1) // 2

    lax.fori_loop(0, NZ, unpack, 0)
    kvg_ref[:, :PROMPT_DEV] = (kacc_ref[...] * SCALE).astype(BF16)
    kvg_ref[:, PROMPT_DEV:] = vacc_ref[...].astype(BF16)
    rg_ref[0] = racc_ref[0] * SCALE
    rg_ref[1] = racc_ref[1]


def shards(
    queries, out_grad, resp_keys, resp_values, prompt_keys, prompt_values, resp_lengths, resp_order
):
    vmem = pl.BlockSpec(memory_space=pltpu.VMEM)
    smem = pl.BlockSpec(memory_space=pltpu.SMEM)
    params = pltpu.CompilerParams(vmem_limit_bytes=48 * 1024 * 1024)
    kv = lax.all_gather(jnp.concatenate([prompt_keys, prompt_values], axis=0), ("yh", "c"))
    resp = lax.all_gather(jnp.stack([resp_keys, resp_values]), "c", axis=1, tiled=True)
    both = jnp.stack(
        [queries.reshape(KVH, GROUP, HD), out_grad.reshape(KVH, GROUP, HD)], axis=1
    )
    both = lax.all_to_all(both, "head", 0, 0, tiled=True)
    both = both.transpose(1, 0, 2, 3).reshape(2, BLOCK, HD)
    rows = lax.all_to_all(
        jnp.broadcast_to(both[None], (NZ, 2, BLOCK, HD)), "z", 0, 0, tiled=True
    )
    packed = jax.ShapeDtypeStruct((CLASS + BLOCK, HD), BF16)
    q, g, info, stat = pl.pallas_call(
        first_kernel,
        out_shape=(packed, packed, packed, jax.ShapeDtypeStruct((2 * CHUNKS, CHUNK), F32)),
        in_specs=[smem, smem, vmem, vmem, vmem],
        out_specs=(vmem, vmem, vmem, vmem),
        compiler_params=params,
        name="first_pass",
    )(resp_lengths, resp_order, rows, kv, resp)
    stats = lax.all_to_all(
        jnp.broadcast_to(stat[None], (NZ,) + stat.shape), "z", 0, 0, tiled=True
    )
    accum = pltpu.VMEM((SHARDS, PROMPT_DEV, HD), F32)
    qg, kvg, rg = pl.pallas_call(
        second_kernel,
        out_shape=(
            jax.ShapeDtypeStruct((CLASS, HD), BF16),
            jax.ShapeDtypeStruct((SHARDS, 2 * PROMPT_DEV, HD), BF16),
            jax.ShapeDtypeStruct((2, 2 * ROWS, HD), F32),
        ),
        in_specs=[smem, smem] + [vmem] * 6,
        out_specs=(vmem, vmem, vmem),
        scratch_shapes=[
            pltpu.VMEM((2 * CHUNKS, CHUNK), F32),
            pltpu.VMEM((SHARDS, HD, PROMPT_DEV), BF16),
            accum,
            accum,
            pltpu.VMEM((2, 2 * ROWS, HD), F32),
            pltpu.VMEM((CLASS + BLOCK, HD), F32),
        ],
        compiler_params=params,
        name="second_pass",
    )(resp_lengths, resp_order, stats, q, g, info, kv, resp)
    terms = lax.all_to_all(
        qg.reshape(NZ * KVH, GROUP, HD), ("z", "head"), 0, 0, tiled=True
    )
    query_grad = (
        jnp.sum(terms.reshape(NZ, QH, HD), axis=0, dtype=F32).astype(BF16).reshape(1, QH * HD)
    )
    c = lax.axis_index("c")
    yh = lax.axis_index("yh")
    swap = [(0, 1), (1, 0)]
    kvg = kvg.reshape(2, 2, 2 * PROMPT_DEV, HD)
    mine = lax.dynamic_index_in_dim(kvg, c, 1, keepdims=False)
    other = lax.dynamic_index_in_dim(kvg, 1 - c, 1, keepdims=False)
    mine = mine.astype(F32) + lax.ppermute(other, "c", swap)
    near = lax.dynamic_index_in_dim(mine, yh, 0, keepdims=False)
    far = lax.dynamic_index_in_dim(mine, 1 - yh, 0, keepdims=False).astype(BF16)
    grads = (near + lax.ppermute(far, "yh", swap)).astype(BF16)
    rg = rg.reshape(2, 2, ROWS, HD)
    resp_mine = lax.dynamic_index_in_dim(rg, c, 1, keepdims=False)
    resp_other = lax.dynamic_index_in_dim(rg, 1 - c, 1, keepdims=False)
    resp_grads = (resp_mine + lax.ppermute(resp_other, "c", swap)).astype(BF16)
    return (
        query_grad,
        grads[:PROMPT_DEV],
        grads[PROMPT_DEV:],
        resp_grads[0],
        resp_grads[1],
    )


def solution(mesh):
    fine = Mesh(mesh.devices.reshape(2, NZ, 2, KVH), ("yh", "z", "c", "head"))
    ctx = ("yh", "z", "c")
    row = P(ctx + ("head",), None)
    col = P(ctx, "head")
    return jax.shard_map(
        shards,
        mesh=fine,
        in_specs=(row, row, col, col, col, col, P(), P()),
        out_specs=(row, col, col, col, col),
        check_vma=False,
    )
```

time: 1170 us -> 155 us (0.13)
  blocking collectives: 538 us -> 12.2 us
  waiting for transfers between devices: 472 us -> 54.1 us
  local copies, waits for them, and re-layouts: 72.6 us -> 12.2 us
  matrix products: 40.6 us -> 0 us
  starting transfers between devices: 5.81 us -> 37.2 us
  other arithmetic: 27.8 us -> 7.23 us
  Pallas kernels: 0 us -> 16.7 us
    all_gather x2 -> x1, waiting for transfers between devices: 266 us -> 0.01 us  [shards(): lax.all_gather(jnp.concatenate([prompt_keys, prompt_values], axis=0), ('y...]
    psum x1 -> x0, blocking collectives: 260 us -> none  [shards(): total, inner = lax.psum((totals * factor, inners * factor), 'ctx')]
    pmax x1 -> x0, blocking collectives: 259 us -> none  [shards(): top = lax.pmax(tops, 'ctx')]
    reduce_scatter x1 -> x0, waiting for transfers between devices: 202 us -> none  [shards(): lax.psum_scatter(q_terms, 'ctx', scatter_dimension=0, tiled=True)]
    all_to_all x1 -> x3, waiting for transfers between devices: 4.18 us -> 54.1 us  [the longest x1 25.2 us: shards(): lax.all_to_all(jnp.broadcast_to(both[None], (NZ, 2, BLOCK, HD)), 'z', 0,...]
    dot_general x56 -> x0, matrix products: 40.6 us -> none  [the longest x16 12.4 us: logits_of(): jnp.einsum('rjgd,kjd->jrgk', q_blk, keys, preferred_element_type=jnp.floa...]
    all_to_all x1 -> x3, starting transfers between devices: 5.68 us -> 29.7 us  [the longest x1 15.2 us: shards(): lax.all_to_all(jnp.broadcast_to(both[None], (NZ, 2, BLOCK, HD)), 'z', 0,...]
    while x16 -> x0, local copies, waits for them, and re-layouts: 21.8 us -> none
  transfers between devices with their start and end apart: 4 -> 7, of which waited for: 4 -> 3; matrix products, arithmetic and copies ran while one was open for 1% -> 5% of each run, Pallas kernels for 0% -> 0%
where the time goes in v1:
time: 155 us; the launch traced here: 154 us
  waiting for transfers between devices  54.1 us (35%)
  starting transfers between devices  37.2 us (24%)
  Pallas kernels  16.7 us (11%)
  between operations  14.2 us (9%)
  local copies, waits for them, and re-layouts  12.2 us (8%)
  blocking collectives  12.2 us (8%)
  other arithmetic  7.23 us (5%)
    all_to_all x1, waiting for transfers between devices, shards(): lax.all_to_all(jnp.broadcast_to(both[None], (NZ, 2, BLOCK, HD)), 'z', 0,...  25.2 us
    all_to_all x1, waiting for transfers between devices, shards(): lax.all_to_all(qg.reshape(NZ * KVH, GROUP, HD), ('z', 'head'), 0, 0, tile...  15.6 us
    all_to_all x1, starting transfers between devices, shards(): lax.all_to_all(jnp.broadcast_to(both[None], (NZ, 2, BLOCK, HD)), 'z', 0,...  15.2 us
    all_to_all x1, waiting for transfers between devices, shards(): lax.all_to_all(jnp.broadcast_to(stat[None], (NZ,) + stat.shape), 'z', 0,...  13.3 us
    pallas_call x1, Pallas kernels, shards(): pl.pallas_call(second_kernel, out_shape=(jax.ShapeDtypeStruct((CLASS, HD)...  11.4 us
    all_to_all x1, blocking collectives, shards(): both = lax.all_to_all(both, 'head', 0, 0, tiled=True)  10.4 us
    unnamed x33, local copies, waits for them, and re-layouts  8.01 us
    all_to_all x1, starting transfers between devices, shards(): lax.all_to_all(qg.reshape(NZ * KVH, GROUP, HD), ('z', 'head'), 0, 0, tile...  7.48 us
  transfers between devices with their start and end apart: 7, of which 3 were waited for; matrix products, arithmetic and copies ran while one was open for 5% of the time, Pallas kernels for 0%

profile of v1, /device:TPU:24, one launch (start us, length us, event | category | flops | bytes accessed | tf_op | source)
XLA Modules:
  0.0 153.8 jit_solution(11550187297812064)
XLA Ops:
  7.2 0.0 copy-start.15
  7.2 0.0 copy-start.10
  7.2 0.0 copy-start.12
  7.2 0.0 all-gather.3.cloned.1.call-start
  7.3 1.8 %pad_maximum_fusion = bf16[1536,128]{1,0:T(8,128)(2,1)} fusion(bf16[768,128]{1,0:T(8,128)(2,1)} %param.13, bf16[768,128]{1,0:T(8,128)(2,1)} %param.12), kind=kLoop, calls=%fused_computation.6 | loop fusion | flops 786432 | bytes 786432 | tf_op jit(solution)/shard_map/concatenate | solution.py:194
  9.0 0.0 all-gather.3.cloned.1.call-update
  9.1 0.8 reduce.1
  9.9 0.8 reduce.2
  10.8 10.4 %all_to_all.20 = bf16[8,2,8,128]{3,2,1,0:T(8,128)(2,1)S(1)} all-to-all(bf16[8,2,8,128]{3,2,1,0:T(8,128)(2,1)S(1)} %pad_maximum_fusion.1), channel_id=1, replica_groups=mesh['yh'=2,'z'=16,'c'=2,'head'=8] {'head'}, dimensions={0} | all-to-all | bytes 65536 | tf_op jit(solution)/shard_map/all_to_all | solution.py:199
  21.2 0.9 broadcast_in_dim.14
  22.1 15.2 %all-to-all-start.1 = ((bf16[16,2,64,128]{3,2,1,0:T(8,128)(2,1)}), bf16[16,2,64,128]{3,2,1,0:T(8,128)(2,1)S(1)}, u32[]{:S(2)}, u32[]{:S(2)}) async-start(bf16[16,2,64,128]{3,2,1,0:T(8,128)(2,1)} %broadcast_in_dim.14), calls=%async_computation.1 | async-start | bytes 1048576 | tf_op jit(solution)/shard_map/all_to_all | solution.py:201
  37.3 0.0 copy-done.15
  37.3 0.0 copy-done.14
  37.3 1.8 %all_gather.11.resp_ref = bf16[2,16,128]{2,1,0:T(8,128)(2,1)S(1)} all-gather(bf16[2,8,128]{2,1,0:T(8,128)(2,1)S(1)} %pad_maximum_fusion.2), channel_id=1, replica_groups=mesh['yh'=2,'z'=16,'c'=2,'head'=8] {'c'}, dimensions={1}, use_global_device_ids=true | all-gather | bytes 12288 | tf_op jit(solution)/shard_map/all_gather | solution.py:195
  39.1 25.2 %all-to-all-done.1.rows_ref = bf16[16,2,64,128]{3,2,1,0:T(8,128)(2,1)S(1)} async-done(((bf16[16,2,64,128]{3,2,1,0:T(8,128)(2,1)}), bf16[16,2,64,128]{3,2,1,0:T(8,128)(2,1)S(1)}, u32[]{:S(2)}, u32[]{:S(2)}) %all-to-all-start.1) | async-done | bytes 524320 | tf_op jit(solution)/shard_map/all_to_all | solution.py:201
  64.3 0.0 copy-done.10
  64.3 1.4 copy-done
  65.7 5.3 %first_pass.1 = (bf16[1088,128]{1,0:T(8,128)(2,1)S(1)}, bf16[1088,128]{1,0:T(8,128)(2,1)S(1)}, bf16[1088,128]{1,0:T(8,128)(2,1)S(1)}, f32[8,256]{1,0:T(8,128)S(1)}) custom-call(s32[16]{0:T(128)S(1)} %copy-done.10, s32[16]{0:T(128)S(1)} %copy-done.12, bf16[16,2,64,128]{3,2,1,0:T(8,128)(2,1)S(1)} %all-to-all-done.1.rows_ref, ...), custom_call_target="tpu_custom_call" | custom-call | tf_op jit(solution)/shard_map/first_pass/pallas_call | solution.py:205
  71.0 0.0 copy-start.2
  71.0 0.7 copy-done.2
  71.8 0.7 copy-done.4
  72.5 0.7 broadcast_in_dim.15
  73.1 7.0 %all-to-all-start.2 = ((f32[16,8,256]{2,1,0:T(8,128)}), f32[16,8,256]{2,1,0:T(8,128)S(1)}, u32[]{:S(2)}, u32[]{:S(2)}) async-start(f32[16,8,256]{2,1,0:T(8,128)} %broadcast_in_dim.15), calls=%async_computation.2 | async-start | bytes 262144 | tf_op jit(solution)/shard_map/all_to_all | solution.py:213
  80.1 13.3 %all-to-all-done.2.stats_ref = f32[16,8,256]{2,1,0:T(8,128)S(1)} async-done(((f32[16,8,256]{2,1,0:T(8,128)}), f32[16,8,256]{2,1,0:T(8,128)S(1)}, u32[]{:S(2)}, u32[]{:S(2)}) %all-to-all-start.2) | async-done | bytes 131104 | tf_op jit(solution)/shard_map/all_to_all | solution.py:213
  93.4 0.0 copy-done.1
  93.4 1.0 copy-done.3
  94.3 1.0 copy-done.5
  95.3 0.7 copy-done.7
  96.0 0.7 copy-done.11
  96.6 0.7 copy-done.13
  97.3 11.4 %second_pass.1 = (bf16[1024,128]{1,0:T(8,128)(2,1)}, bf16[4,1536,128]{2,1,0:T(8,128)(2,1)S(1)}, f32[2,16,128]{2,1,0:T(8,128)S(1)}) custom-call(s32[16]{0:T(128)S(1)} %copy-done.11, s32[16]{0:T(128)S(1)} %copy-done.13, f32[16,8,256]{2,1,0:T(8,128)S(1)} %all-to-all-done.2.stats_ref, bf16[1088,128]{1,0:T(8,128)(2,1)S(1)} %get-tuple-element.13.q_ref, ...), custom_call_target="tpu_custom_call" | custom-call | tf_op jit(solution)/shard_map/second_pass/pallas_call | solution.py:217
  108.7 0.6 copy-done.8
  109.3 0.1 dynamic-slice_bitcast_fusion
  109.4 1.9 %collective-permute-start = (bf16[2,1536,128]{2,1,0:T(8,128)(2,1)S(1)}, bf16[2,1536,128]{2,1,0:T(8,128)(2,1)}, u32[]{:S(2)}, u32[]{:S(2)}) collective-permute-start(bf16[2,1536,128]{2,1,0:T(8,128)(2,1)S(1)} %dynamic-slice_bitcast_fusion), channel_id=1, source_target_pairs={{0,8},{8,0},{1,9},{9,1},{2,10},{10,2},{3,11},{11,3},{4,12},{12,4},... | collective-permute-start | bytes 2359304 | tf_op jit(solution)/shard_map/ppermute | solution.py:249
  111.3 0.0 copy-done.9
  111.3 2.4 %collective-permute-start.2 = (f32[2,8,128]{2,1,0:T(8,128)S(1)}, f32[2,8,128]{2,1,0:T(8,128)S(1)}, u32[]{:S(2)}, u32[]{:S(2)}) collective-permute-start(f32[2,8,128]{2,1,0:T(8,128)S(1)} %dynamic-slice_bitcast_fusion.1), channel_id=1, source_target_pairs={{0,8},{8,0},{1,9},{9,1},{2,10},{10,2},{3,11},{11,3},{4,12},{12,4},... | collective-permute-start | bytes 24584 | tf_op jit(solution)/shard_map/ppermute | solution.py:256
  113.8 7.5 %all-to-all-start.3 = ((bf16[128,8,128]{2,1,0:T(8,128)(2,1)}), bf16[128,8,128]{2,1,0:T(8,128)(2,1)S(1)}, u32[]{:S(2)}, u32[]{:S(2)}) async-start(bf16[128,8,128]{2,1,0:T(8,128)(2,1)} %bitcast.5), calls=%async_computation.3 | async-start | bytes 524288 | tf_op jit(solution)/shard_map/all_to_all | solution.py:237
  121.2 0.0 collective-permute-done
  121.3 2.5 %convert_add_fusion = f32[2,1536,128]{2,1,0:T(8,128)} fusion(bf16[2,1536,128]{2,1,0:T(8,128)(2,1)} %collective-permute-done, bf16[2,2,1536,128]{3,2,1,0:T(8,128)(2,1)S(1)} %bitcast.47, s32[]{:T(128)S(6)} %select_n.17), kind=kLoop, calls=%fused_computation | loop fusion | flops 1179648 | bytes 3145732 | tf_op jit(solution)/shard_map/add | solution.py:249
  123.7 1.2 fusion.1
  124.9 3.1 %collective-permute-start.1 = (bf16[1536,128]{1,0:T(8,128)(2,1)S(1)}, bf16[1536,128]{1,0:T(8,128)(2,1)S(1)}, u32[]{:S(2)}, u32[]{:S(2)}) collective-permute-start(bf16[1536,128]{1,0:T(8,128)(2,1)S(1)} %fusion.1), channel_id=1, source_target_pairs={{0,256},{256,0},{1,257},{257,1},{2,258},{258,2},{3,259},{259,3},{4... | collective-permute-start | bytes 1179656 | tf_op jit(solution)/shard_map/ppermute | solution.py:252
  128.0 0.0 collective-permute-done.2
  128.1 0.6 slice_bitcast_fusion
  128.7 15.6 %all-to-all-done.3 = bf16[128,8,128]{2,1,0:T(8,128)(2,1)S(1)} async-done(((bf16[128,8,128]{2,1,0:T(8,128)(2,1)}), bf16[128,8,128]{2,1,0:T(8,128)(2,1)S(1)}, u32[]{:S(2)}, u32[]{:S(2)}) %all-to-all-start.3) | async-done | bytes 262176 | tf_op jit(solution)/shard_map/all_to_all | solution.py:237
  144.3 0.6 copy.21
  145.0 0.0 collective-permute-done.1
  145.0 1.2 fusion
  146.2 0.8 fusion.3
  (21 shorter events, 0.1 us)
Async XLA Ops:
  7.2 30.1 %copy-start.15 = (bf16[8,128]{1,0:T(8,128)(2,1)S(1)}, bf16[8,128]{1,0:T(8,128)(2,1)}, u32[]{:S(2)}) copy-start(bf16[8,128]{1,0:T(8,128)(2,1)} %param.10) | copy-start | bytes 6148
  7.2 30.1 %copy-start.14 = (bf16[8,128]{1,0:T(8,128)(2,1)S(1)}, bf16[8,128]{1,0:T(8,128)(2,1)}, u32[]{:S(2)}) copy-start(bf16[8,128]{1,0:T(8,128)(2,1)} %param.11) | copy-start | bytes 6148
  7.2 57.1 %copy-start.10 = (s32[16]{0:T(128)S(1)}, s32[16]{0:T(128)}, u32[]{:S(2)}) copy-start(s32[16]{0:T(128)} %lengths_ref.3) | copy-start | bytes 196
  7.2 57.1 %copy-start.12 = (s32[16]{0:T(128)S(1)}, s32[16]{0:T(128)}, u32[]{:S(2)}) copy-start(s32[16]{0:T(128)} %order_ref.3) | copy-start | bytes 196
  7.2 57.1 %all-gather.3.cloned.1.call-start = ((), (), s32[]{:S(2)}) async-start(), calls=%async_computation.4 | async-start | bytes 1966080 | tf_op jit(solution)/shard_map/all_gather | solution.py:194
  22.1 42.2 %all-to-all-start.1 = ((bf16[16,2,64,128]{3,2,1,0:T(8,128)(2,1)}), bf16[16,2,64,128]{3,2,1,0:T(8,128)(2,1)S(1)}, u32[]{:S(2)}, u32[]{:S(2)}) async-start(bf16[16,2,64,128]{3,2,1,0:T(8,128)(2,1)} %broadcast_in_dim.14), calls=%async_computation.1 | async-start | bytes 1048576 | tf_op jit(solution)/shard_map/all_to_all | solution.py:201
  39.1 54.2 %copy-start.6 = (bf16[2,16,128]{2,1,0:T(8,128)(2,1)}, bf16[2,16,128]{2,1,0:T(8,128)(2,1)S(1)}, u32[]{:S(2)}) copy-start(bf16[2,16,128]{2,1,0:T(8,128)(2,1)S(1)} %all_gather.11.resp_ref) | copy-start | bytes 24580
  64.3 1.4 copy-start
  65.7 27.7 %copy-start.1 = (bf16[6144,128]{1,0:T(8,128)(2,1)S(1)}, bf16[6144,128]{1,0:T(8,128)(2,1)}, u32[]{:S(2)}) copy-start(bf16[6144,128]{1,0:T(8,128)(2,1)} %all-gather.3.cloned.1.call-done) | copy-start | bytes 4718596
  71.0 0.7 copy-start.2
  71.7 0.7 copy-start.4
  73.1 20.2 %all-to-all-start.2 = ((f32[16,8,256]{2,1,0:T(8,128)}), f32[16,8,256]{2,1,0:T(8,128)S(1)}, u32[]{:S(2)}, u32[]{:S(2)}) async-start(f32[16,8,256]{2,1,0:T(8,128)} %broadcast_in_dim.15), calls=%async_computation.2 | async-start | bytes 262144 | tf_op jit(solution)/shard_map/all_to_all | solution.py:213
  93.4 1.0 copy-start.3
  94.3 1.0 copy-start.5
  95.3 0.7 copy-start.7
  96.0 0.7 copy-start.11
  96.6 0.7 copy-start.13
  108.7 0.6 copy-start.8
  109.3 2.0 %copy-start.9 = (f32[2,16,128]{2,1,0:T(8,128)S(1)}, f32[2,16,128]{2,1,0:T(8,128)}, u32[]{:S(2)}) copy-start(f32[2,16,128]{2,1,0:T(8,128)} %copy-done.8) | copy-start | bytes 49156
  109.4 11.9 %collective-permute-start = (bf16[2,1536,128]{2,1,0:T(8,128)(2,1)S(1)}, bf16[2,1536,128]{2,1,0:T(8,128)(2,1)}, u32[]{:S(2)}, u32[]{:S(2)}) collective-permute-start(bf16[2,1536,128]{2,1,0:T(8,128)(2,1)S(1)} %dynamic-slice_bitcast_fusion), channel_id=1, source_target_pairs={{0,8},{8,0},{1,9},{9,1},{2,10},{10,2},{3,11},{11,3},{4,12},{12,4},... | collective-permute-start | bytes 2359304 | tf_op jit(solution)/shard_map/ppermute | solution.py:249
  111.3 16.7 %collective-permute-start.2 = (f32[2,8,128]{2,1,0:T(8,128)S(1)}, f32[2,8,128]{2,1,0:T(8,128)S(1)}, u32[]{:S(2)}, u32[]{:S(2)}) collective-permute-start(f32[2,8,128]{2,1,0:T(8,128)S(1)} %dynamic-slice_bitcast_fusion.1), channel_id=1, source_target_pairs={{0,8},{8,0},{1,9},{9,1},{2,10},{10,2},{3,11},{11,3},{4,12},{12,4},... | collective-permute-start | bytes 24584 | tf_op jit(solution)/shard_map/ppermute | solution.py:256
  113.8 30.5 %all-to-all-start.3 = ((bf16[128,8,128]{2,1,0:T(8,128)(2,1)}), bf16[128,8,128]{2,1,0:T(8,128)(2,1)S(1)}, u32[]{:S(2)}, u32[]{:S(2)}) async-start(bf16[128,8,128]{2,1,0:T(8,128)(2,1)} %bitcast.5), calls=%async_computation.3 | async-start | bytes 524288 | tf_op jit(solution)/shard_map/all_to_all | solution.py:237
  124.9 20.1 %collective-permute-start.1 = (bf16[1536,128]{1,0:T(8,128)(2,1)S(1)}, bf16[1536,128]{1,0:T(8,128)(2,1)S(1)}, u32[]{:S(2)}, u32[]{:S(2)}) collective-permute-start(bf16[1536,128]{1,0:T(8,128)(2,1)S(1)} %fusion.1), channel_id=1, source_target_pairs={{0,256},{256,0},{1,257},{257,1},{2,258},{258,2},{3,259},{259,3},{4... | collective-permute-start | bytes 1179656 | tf_op jit(solution)/shard_map/ppermute | solution.py:252
Sparse Core Ops, SparseCore 0:
  10.2 33.9 all-gather.2

commit v2 on v1

v2 whole, which is shorter than its diff:
```python
import math

import jax
import jax.numpy as jnp
from jax import lax
from jax.experimental import pallas as pl
from jax.experimental.pallas import tpu as pltpu
from jax.sharding import Mesh
from jax.sharding import PartitionSpec as P

QH = 64
KVH = 8
HD = 128
NRESP = 16
GROUP = QH // KVH
SLOT = 32
NZ = 16
ROWS = 8
BLOCK = ROWS * GROUP
CLASS = NZ * BLOCK
CHUNK = 256
CHUNKS = CLASS // CHUNK
PROMPT_DEV = 768
KEYS = 384
OWN_KEYS = 256
WIDE = 2
SCALE = 1.0 / math.sqrt(HD)
SCALE2 = SCALE * math.log2(math.e)
F32 = jnp.float32
BF16 = jnp.bfloat16


def nt(a, b):
    return lax.dot_general(a, b, (((1,), (1,)), ((), ())), preferred_element_type=F32)


def nn(a, b):
    return jnp.dot(a, b, preferred_element_type=F32)


def live_rows(lengths_ref, order_ref, yh, c, z):
    length = lengths_ref[order_ref[yh * (NRESP // 2) + z // 2]]
    return jnp.clip(length - ((z % 2) * 2 + c) * ROWS, 0, ROWS)


def pack_rows(lengths_ref, order_ref, rows_ref, yh, c, near, start, q_ref, g_ref, info_ref):
    in_block = lax.broadcasted_iota(jnp.int32, (BLOCK, HD), 0)
    at = start * (CHUNK // 16)
    for z in range(NZ):
        live = live_rows(lengths_ref, order_ref, yh, c, z)
        place = pl.ds(pl.multiple_of(at * 16, 16), BLOCK)
        both = rows_ref[z * ROWS : (z + 1) * ROWS].astype(F32)
        q_ref[place] = both[:, :GROUP].reshape(BLOCK, HD).astype(BF16)
        g = both[:, GROUP:].reshape(BLOCK, HD)
        g_ref[place] = jnp.where(in_block < live * GROUP, g, 0.0).astype(BF16)
        if near:
            code = (z // 2) * SLOT + ((z % 2) * 2 + c) * ROWS + in_block // GROUP
            info_ref[place] = code.astype(F32).astype(BF16)
        at = at + (live + 1) // 2
    rest = pl.ds(pl.multiple_of(at * 16, 16), 2 * CHUNK)
    q_ref[rest] = jnp.zeros((2 * CHUNK, HD), BF16)
    g_ref[rest] = jnp.zeros((2 * CHUNK, HD), BF16)
    if near:
        info_ref[rest] = jnp.full((2 * CHUNK, HD), -SLOT, BF16)
    return (at * 16 + CHUNK - 1) // CHUNK


def unpack_rows(lengths_ref, order_ref, yh, c, acc_ref, out_ref):
    in_block = lax.broadcasted_iota(jnp.int32, (BLOCK, HD), 0)
    at = 0
    for z in range(NZ):
        live = live_rows(lengths_ref, order_ref, yh, c, z)
        block = acc_ref[pl.ds(pl.multiple_of(at * 16, 16), BLOCK)]
        out_ref[z * BLOCK : (z + 1) * BLOCK] = jnp.where(
            in_block < live * GROUP, block, 0.0
        ).astype(BF16)
        at = at + (live + 1) // 2


def key_code(z, c):
    at = lax.broadcasted_iota(jnp.int32, (ROWS, 1), 0)
    return (z // 2) * SLOT + ((z % 2) * 2 + c) * ROWS + at


def row_code(info):
    first = (lax.broadcasted_iota(jnp.int32, (16, HD), 1) == 0).astype(BF16)
    return nt(first, info)[:1].astype(jnp.int32)


def seen_of(rows, keys):
    return (rows >= keys) & (rows < (keys // SLOT + 1) * SLOT)


def stack8(a, b):
    return jnp.concatenate([a.astype(F32), b.astype(F32)], axis=0).astype(BF16)


def send_kernel(q_hbm, g_hbm, rows_ref, q_ref, g_ref, hold_ref, sems):
    copies = [
        pltpu.make_async_copy(q_hbm, q_ref, sems.at[0]),
        pltpu.make_async_copy(g_hbm, g_ref, sems.at[1]),
    ]
    for copy in copies:
        copy.start()
    for copy in copies:
        copy.wait()
    for h in range(QH):
        at = slice(h * HD, (h + 1) * HD)
        hold_ref[h // GROUP, h % GROUP : h % GROUP + 1] = q_ref[:, at].astype(F32)
        hold_ref[h // GROUP, GROUP + h % GROUP : GROUP + h % GROUP + 1] = g_ref[:, at].astype(F32)
    for z in range(NZ):
        rows_ref[z * KVH : (z + 1) * KVH] = hold_ref[...].astype(BF16)


def keys_kernel(k_hbm, v_hbm, rk_hbm, rv_hbm, kv_ref, rk_ref, rv_ref, sems):
    copies = [
        pltpu.make_async_copy(k_hbm, kv_ref.at[:PROMPT_DEV], sems.at[0]),
        pltpu.make_async_copy(v_hbm, kv_ref.at[PROMPT_DEV : 2 * PROMPT_DEV], sems.at[1]),
        pltpu.make_async_copy(rk_hbm, rk_ref, sems.at[2]),
        pltpu.make_async_copy(rv_hbm, rv_ref, sems.at[3]),
    ]
    for copy in copies:
        copy.start()
    for copy in copies:
        copy.wait()
    kv_ref[2 * PROMPT_DEV :] = stack8(rk_ref[...], rv_ref[...])


def resp_of(kv_ref):
    a, b = (kv_ref[c, 2 * PROMPT_DEV :].astype(F32) for c in range(2))
    keys = jnp.concatenate([a[:ROWS], b[:ROWS]], axis=0).astype(BF16)
    values = jnp.concatenate([a[ROWS:], b[ROWS:]], axis=0).astype(BF16)
    return keys, values


def lanes_of(ref, first, count):
    return jnp.concatenate([ref[i : i + 1] for i in range(first, first + count)], axis=1)


def key_parts(near_ref, far_ref):
    return [
        (ref, c, b) for ref in (near_ref, far_ref) for c in range(2) for b in range(0, PROMPT_DEV, KEYS)
    ]


def first_kernel(
    lengths_ref,
    order_ref,
    rows_ref,
    near_kv_ref,
    far_kv_ref,
    out_ref,
    stat_ref,
    q_ref,
    g_ref,
    info_ref,
    near_ref,
):
    yh, c, z = lax.axis_index("yh"), lax.axis_index("c"), lax.axis_index("z")
    chunks = pack_rows(
        lengths_ref, order_ref, rows_ref, yh, c, True, 0, q_ref, g_ref, info_ref
    )
    stat_ref[...] = jnp.zeros_like(stat_ref)
    resp_k, resp_v = resp_of(near_kv_ref)
    keys = jnp.concatenate([key_code(z, 0), key_code(z, 1)], axis=0)
    seen = seen_of(row_code(info_ref[:CLASS]), keys)
    logits = jnp.where(seen, nt(resp_k, q_ref[:CLASS]) * SCALE2, -1e30)
    top = jnp.maximum(jnp.max(logits, axis=0, keepdims=True), -1e29)
    weights = jnp.exp2(logits - top)
    total = jnp.sum(weights, axis=0, keepdims=True)
    inner = jnp.sum(weights * nt(resp_v, g_ref[:CLASS]), axis=0, keepdims=True)
    for i in range(CHUNKS):
        lanes = slice(i * CHUNK, (i + 1) * CHUNK)
        near_ref[0, i : i + 1] = top[:, lanes]
        near_ref[1, i : i + 1] = total[:, lanes]
        near_ref[2, i : i + 1] = inner[:, lanes]

    def chunk(i, _):
        place = pl.ds(pl.multiple_of(i * CHUNK, CHUNK), CHUNK)
        q, g = q_ref[place], g_ref[place]
        top, total, inner = (near_ref[n, pl.ds(i, 1)] for n in range(3))
        for ref, k, b in key_parts(near_kv_ref, far_kv_ref):
            logits = nt(ref[k, b : b + KEYS], q) * SCALE2
            dprob = nt(ref[k, PROMPT_DEV + b : PROMPT_DEV + b + KEYS], g)
            now = jnp.maximum(top, jnp.max(logits, axis=0, keepdims=True))
            weights = jnp.exp2(logits - now)
            factor = jnp.exp2(top - now)
            total = total * factor + jnp.sum(weights, axis=0, keepdims=True)
            inner = inner * factor + jnp.sum(weights * dprob, axis=0, keepdims=True)
            top = now
        stat_ref[pl.ds(i, 1)] = top + jnp.log2(total)
        stat_ref[pl.ds(CHUNKS + i, 1)] = inner / total
        return 0

    lax.fori_loop(0, chunks, chunk, 0)
    for n in range(NZ):
        out_ref[n] = stat_ref[...]


def query_kernel(
    lengths_ref,
    order_ref,
    stats_ref,
    rows_ref,
    near_kv_ref,
    far_kv_ref,
    mix_ref,
    qg_ref,
    q_ref,
    g_ref,
    info_ref,
    near_ref,
    keyt_ref,
    qacc_ref,
):
    yh, c, z = lax.axis_index("yh"), lax.axis_index("c"), lax.axis_index("z")
    logs = stats_ref[:, :CHUNKS]
    top = jnp.max(logs, axis=0)
    weights = jnp.exp2(logs - top[None])
    total = jnp.sum(weights, axis=0)
    mix_ref[:CHUNKS] = top + jnp.log2(total)
    mix_ref[CHUNKS:] = jnp.sum(weights * stats_ref[:, CHUNKS:], axis=0) / total
    for n, (ref, k, b) in enumerate(key_parts(near_kv_ref, far_kv_ref)):
        keyt_ref[n] = ref[k, b : b + KEYS].T
    chunks = pack_rows(
        lengths_ref, order_ref, rows_ref, yh, c, True, 0, q_ref, g_ref, info_ref
    )
    resp_k, resp_v = resp_of(near_kv_ref)
    keys = jnp.concatenate([key_code(z, 0), key_code(z, 1)], axis=0)
    seen = seen_of(row_code(info_ref[:CLASS]), keys)
    log, delta = lanes_of(mix_ref, 0, CHUNKS), lanes_of(mix_ref, CHUNKS, CHUNKS)
    prob = jnp.exp2(jnp.where(seen, nt(resp_k, q_ref[:CLASS]) * SCALE2 - log, -1e30))
    near_ref[...] = (prob * (nt(resp_v, g_ref[:CLASS]) - delta)).astype(BF16).T

    def chunk(i, _):
        place = pl.ds(pl.multiple_of(i * CHUNK, CHUNK), CHUNK)
        q, g = q_ref[place], g_ref[place]
        log, delta = mix_ref[pl.ds(i, 1)], mix_ref[pl.ds(CHUNKS + i, 1)]
        qgrad = jnp.zeros((HD, CHUNK), F32)
        for n, (ref, k, b) in enumerate(key_parts(near_kv_ref, far_kv_ref)):
            prob = jnp.exp2(nt(ref[k, b : b + KEYS], q) * SCALE2 - log)
            dprob = nt(ref[k, PROMPT_DEV + b : PROMPT_DEV + b + KEYS], g)
            qgrad = qgrad + nn(keyt_ref[n], (prob * (dprob - delta)).astype(BF16))
        qacc_ref[place] = (qgrad.T + nn(near_ref[place], resp_k)) * SCALE
        return 0

    lax.fori_loop(0, chunks, chunk, 0)
    unpack_rows(lengths_ref, order_ref, yh, c, qacc_ref, qg_ref)


def key_kernel(
    lengths_ref,
    order_ref,
    mix_ref,
    rows_ref,
    rows_c_ref,
    rows_y_ref,
    rows_yc_ref,
    own_ref,
    kg_ref,
    vg_ref,
    rkg_ref,
    rvg_ref,
    q_ref,
    g_ref,
    info_ref,
    log_ref,
    delta_ref,
    kacc_ref,
    vacc_ref,
):
    yh, c, z = lax.axis_index("yh"), lax.axis_index("c"), lax.axis_index("z")
    kacc_ref[...] = jnp.zeros_like(kacc_ref)
    vacc_ref[...] = jnp.zeros_like(vacc_ref)
    log_ref[...] = jnp.zeros_like(log_ref)
    delta_ref[...] = jnp.zeros_like(delta_ref)
    chunks = 0
    for far, cross, ref in (
        (0, 0, rows_ref),
        (0, 1, rows_c_ref),
        (1, 0, rows_y_ref),
        (1, 1, rows_yc_ref),
    ):
        its_yh, its_c = (1 - yh if far else yh), (1 - c if cross else c)
        its = its_yh * 2 + its_c
        for i in range(CHUNKS):
            log_ref[pl.ds(chunks + i, 1)] = mix_ref[its, i : i + 1]
            delta_ref[pl.ds(chunks + i, 1)] = mix_ref[its, CHUNKS + i : CHUNKS + i + 1]
        chunks = pack_rows(
            lengths_ref, order_ref, ref, its_yh, its_c, not far, chunks, q_ref, g_ref, info_ref
        )
        if not far:
            info_ref[pl.ds(pl.multiple_of(chunks * CHUNK, CHUNK), CLASS)] = jnp.full(
                (CLASS, HD), -SLOT, BF16
            )
    resp = own_ref[2 * PROMPT_DEV :]
    none = jnp.zeros((ROWS, HD), F32)
    resp_k = jnp.concatenate([resp[:ROWS].astype(F32), none], axis=0).astype(BF16)
    resp_v = jnp.concatenate([resp[ROWS:].astype(F32), none], axis=0).astype(BF16)
    keys = jnp.concatenate([key_code(z, c), jnp.full((ROWS, 1), 1 << 20, jnp.int32)], axis=0)
    seen = seen_of(row_code(info_ref[: 2 * CLASS]), keys)
    log, delta = lanes_of(log_ref, 0, 2 * CHUNKS), lanes_of(delta_ref, 0, 2 * CHUNKS)
    q, g = q_ref[: 2 * CLASS], g_ref[: 2 * CLASS]
    prob = jnp.exp2(jnp.where(seen, nt(resp_k, q) * SCALE2 - log, -1e30))
    dscore = (prob * (nt(resp_v, g) - delta)).astype(BF16)
    rkg_ref[...] = (nn(dscore, q)[:ROWS] * SCALE).astype(BF16)
    rvg_ref[...] = nn(prob.astype(BF16), g)[:ROWS].astype(BF16)

    def step(n, _):
        place = pl.ds(pl.multiple_of(n * WIDE * CHUNK, CHUNK), WIDE * CHUNK)
        q, g = q_ref[place], g_ref[place]
        log = jnp.concatenate([log_ref[pl.ds(WIDE * n + i, 1)] for i in range(WIDE)], axis=1)
        delta = jnp.concatenate([delta_ref[pl.ds(WIDE * n + i, 1)] for i in range(WIDE)], axis=1)
        for b in range(0, PROMPT_DEV, OWN_KEYS):
            prob = jnp.exp2(nt(own_ref[b : b + OWN_KEYS], q) * SCALE2 - log)
            dprob = nt(own_ref[PROMPT_DEV + b : PROMPT_DEV + b + OWN_KEYS], g)
            dscore = (prob * (dprob - delta)).astype(BF16)
            kacc_ref[b : b + OWN_KEYS] += nn(dscore, q)
            vacc_ref[b : b + OWN_KEYS] += nn(prob.astype(BF16), g)
        return 0

    lax.fori_loop(0, (chunks + WIDE - 1) // WIDE, step, 0)
    kg_ref[...] = (kacc_ref[...] * SCALE).astype(BF16)
    vg_ref[...] = vacc_ref[...].astype(BF16)


def finish_kernel(terms_ref, out_ref):
    total = jnp.sum(terms_ref[...].astype(F32), axis=0)
    for h in range(QH):
        out_ref[:, h * HD : (h + 1) * HD] = total[h : h + 1].astype(BF16)


def shards(
    queries, out_grad, resp_keys, resp_values, prompt_keys, prompt_values, resp_lengths, resp_order
):
    vmem = pl.BlockSpec(memory_space=pltpu.VMEM)
    smem = pl.BlockSpec(memory_space=pltpu.SMEM)
    hbm = pl.BlockSpec(memory_space=pltpu.HBM)
    params = pltpu.CompilerParams(vmem_limit_bytes=32 * 1024 * 1024)
    swap = [(0, 1), (1, 0)]
    shape = jax.ShapeDtypeStruct

    def call(kernel, name, out_shape, ints, arrays, scratch=(), space=vmem):
        return pl.pallas_call(
            kernel,
            out_shape=out_shape,
            in_specs=[smem] * len(ints) + [space] * len(arrays),
            out_specs=jax.tree.map(lambda _: vmem, out_shape),
            scratch_shapes=list(scratch),
            compiler_params=params,
            name=name,
        )(*ints, *arrays)

    whole = pltpu.VMEM((1, QH * HD), BF16)
    rows = call(
        send_kernel,
        "send",
        shape((NZ * KVH, 2 * GROUP, HD), BF16),
        (),
        (queries, out_grad),
        [whole, whole, pltpu.VMEM((KVH, 2 * GROUP, HD), F32), pltpu.SemaphoreType.DMA((2,))],
        hbm,
    )
    few = pltpu.VMEM((ROWS, HD), BF16)
    kv = call(
        keys_kernel,
        "keys",
        shape((2 * PROMPT_DEV + 2 * ROWS, HD), BF16),
        (),
        (prompt_keys, prompt_values, resp_keys, resp_values),
        [few, few, pltpu.SemaphoreType.DMA((4,))],
        hbm,
    )
    near_kv = lax.all_gather(kv, "c")
    far_kv = lax.all_gather(lax.ppermute(kv, "yh", swap), "c")
    rows = lax.all_to_all(rows, ("z", "head"), 0, 0, tiled=True)
    packed = pltpu.VMEM((CLASS + BLOCK + 2 * CHUNK, HD), BF16)
    ints = (resp_lengths, resp_order)
    stats = call(
        first_kernel,
        "first_pass",
        shape((NZ, 2 * CHUNKS, CHUNK), F32),
        ints,
        (rows, near_kv, far_kv),
        [
            pltpu.VMEM((2 * CHUNKS, CHUNK), F32),
            packed,
            packed,
            packed,
            pltpu.VMEM((3, 2 * CHUNKS, CHUNK), F32),
        ],
    )
    stats, rows = lax.optimization_barrier((stats, rows))
    rows_c = lax.ppermute(rows, "c", swap)
    rows_y = lax.ppermute(rows, "yh", swap)
    rows_yc = lax.ppermute(rows_y, "c", swap)
    stats = lax.all_to_all(stats, "z", 0, 0, tiled=True)
    stats, rows_c = lax.optimization_barrier((stats, rows_c))
    mix, qg = call(
        query_kernel,
        "query_pass",
        (shape((2 * CHUNKS, CHUNK), F32), shape((CLASS, HD), BF16)),
        ints,
        (stats, rows, near_kv, far_kv),
        [
            packed,
            packed,
            packed,
            pltpu.VMEM((CLASS, 2 * ROWS), BF16),
            pltpu.VMEM((4 * PROMPT_DEV // KEYS, HD, KEYS), BF16),
            pltpu.VMEM((CLASS + BLOCK, HD), F32),
        ],
    )
    terms = lax.all_to_all(
        qg.reshape(NZ * KVH, GROUP, HD), ("z", "head"), 0, 0, tiled=True
    )
    mixes = lax.all_gather(mix, ("yh", "c"))
    acc = pltpu.VMEM((PROMPT_DEV, HD), F32)
    everyone = pltpu.VMEM((4 * CLASS + BLOCK + 2 * CHUNK, HD), BF16)
    per_chunk = pltpu.VMEM((6 * CHUNKS, CHUNK), F32)
    key_grad, value_grad, resp_key_grad, resp_value_grad = call(
        key_kernel,
        "key_pass",
        (
            shape((PROMPT_DEV, HD), BF16),
            shape((PROMPT_DEV, HD), BF16),
            shape((ROWS, HD), BF16),
            shape((ROWS, HD), BF16),
        ),
        ints,
        (mixes, rows, rows_c, rows_y, rows_yc, kv),
        [everyone, everyone, everyone, per_chunk, per_chunk, acc, acc],
    )
    query_grad = call(
        finish_kernel, "finish", shape((1, QH * HD), BF16), (), (terms.reshape(NZ, QH, HD),)
    )
    return query_grad, key_grad, value_grad, resp_key_grad, resp_value_grad


def solution(mesh):
    fine = Mesh(mesh.devices.reshape(2, NZ, 2, KVH), ("yh", "z", "c", "head"))
    ctx = ("yh", "z", "c")
    row = P(ctx + ("head",), None)
    col = P(ctx, "head")
    return jax.shard_map(
        shards,
        mesh=fine,
        in_specs=(row, row, col, col, col, col, P(), P()),
        out_specs=(row, col, col, col, col),
        check_vma=False,
    )
```

time: 155 us -> 123 us (0.79)
  waiting for transfers between devices: 54.1 us -> 38.4 us
  between operations: 14.2 us -> 0.79 us
  local copies, waits for them, and re-layouts: 12.2 us -> 2.2 us
  Pallas kernels: 16.7 us -> 25.7 us
  other arithmetic: 7.23 us -> 0 us
  starting transfers between devices: 37.2 us -> 43.8 us
    all_to_all x2, waiting for transfers between devices: 38.4 us -> 25 us  [the longest x1 14.4 us: shards(): rows = lax.all_to_all(rows, ('z', 'head'), 0, 0, tiled=True)]
    all_to_all x1, waiting for transfers between devices: 15.6 us -> 2.63 us  [shards(): lax.all_to_all(qg.reshape(NZ * KVH, GROUP, HD), ('z', 'head'), 0, 0, tile...]
    ppermute x3 -> x4, waiting for transfers between devices: 0.01 us -> 10.8 us  [the longest x1 10.8 us: shards(): far_kv = lax.all_gather(lax.ppermute(kv, 'yh', swap), 'c')]
    all_to_all x1 -> x0, blocking collectives: 10.4 us -> none  [shards(): both = lax.all_to_all(both, 'head', 0, 0, tiled=True)]
    all_gather x1 -> x3, blocking collectives: 1.8 us -> 11.5 us  [the longest x1 6.72 us: shards(): mixes = lax.all_gather(mix, ('yh', 'c'))]
    pallas_call x2 -> x6, Pallas kernels: 16.7 us -> 25.7 us  [call(): pl.pallas_call(kernel, out_shape=out_shape, in_specs=[smem] * len(ints) +...]
    unnamed x33 -> x16, local copies, waits for them, and re-layouts: 8.01 us -> 2.2 us
    ppermute x3 -> x4, starting transfers between devices: 7.48 us -> 10.1 us  [the longest x1 3.14 us: shards(): far_kv = lax.all_gather(lax.ppermute(kv, 'yh', swap), 'c')]
  transfers between devices with their start and end apart: 7 -> 7, of which waited for: 3 -> 4; matrix products, arithmetic and copies ran while one was open for 5% -> 0% of each run, Pallas kernels for 0% -> 15%
where the time goes in v2:
time: 123 us; the launch traced here: 122 us
  starting transfers between devices  43.8 us (36%)
  waiting for transfers between devices  38.4 us (31%)
  Pallas kernels  25.7 us (21%)
  blocking collectives  11.5 us (9%)
  local copies, waits for them, and re-layouts  2.2 us (2%)
    pallas_call x6, Pallas kernels, call(): pl.pallas_call(kernel, out_shape=out_shape, in_specs=[smem] * len(ints) +...  25.7 us
    all_to_all x1, starting transfers between devices, shards(): rows = lax.all_to_all(rows, ('z', 'head'), 0, 0, tiled=True)  20.5 us
    all_to_all x1, waiting for transfers between devices, shards(): rows = lax.all_to_all(rows, ('z', 'head'), 0, 0, tiled=True)  14.4 us
    ppermute x1, waiting for transfers between devices, shards(): far_kv = lax.all_gather(lax.ppermute(kv, 'yh', swap), 'c')  10.8 us
    all_to_all x1, waiting for transfers between devices, shards(): stats = lax.all_to_all(stats, 'z', 0, 0, tiled=True)  10.7 us
    all_to_all x1, starting transfers between devices, shards(): lax.all_to_all(qg.reshape(NZ * KVH, GROUP, HD), ('z', 'head'), 0, 0, tile...  9.65 us
    all_gather x1, blocking collectives, shards(): mixes = lax.all_gather(mix, ('yh', 'c'))  6.72 us
    all_to_all x1, starting transfers between devices, shards(): stats = lax.all_to_all(stats, 'z', 0, 0, tiled=True)  3.52 us
  transfers between devices with their start and end apart: 7, of which 4 were waited for; matrix products, arithmetic and copies ran while one was open for 0% of the time, Pallas kernels for 15%

profile of v2, /device:TPU:24, one launch (start us, length us, event | category | flops | bytes accessed | tf_op | source)
XLA Modules:
  0.0 122.4 jit_solution(10006577558204042237)
XLA Ops:
  0.6 0.0 copy-start.2
  0.6 0.7 copy-done.2
  1.4 0.0 copy-start.3
  1.4 0.8 copy-done.3
  2.1 1.0 send.1
  3.1 0.0 copy-start
  3.1 0.0 copy-start.1
  3.1 0.0 copy-start.6
  3.2 0.0 copy-start.7
  3.2 20.5 %all-to-all-start = ((bf16[128,16,128]{2,1,0:T(8,128)(2,1)}), bf16[128,16,128]{2,1,0:T(8,128)(2,1)S(1)}, u32[]{:S(2)}, u32[]{:S(2)}) async-start(bf16[128,16,128]{2,1,0:T(8,128)(2,1)} %send.1), calls=%async_computation | async-start | bytes 1048576 | tf_op jit(solution)/shard_map/all_to_all | solution.py:376
  23.7 0.0 copy-done
  23.7 0.0 copy-done.1
  23.7 0.0 copy-done.6
  23.7 0.0 copy-done.7
  23.7 0.6 keys.1.own_ref
  24.3 3.1 %collective-permute-start = (bf16[1552,128]{1,0:T(8,128)(2,1)S(1)}, bf16[1552,128]{1,0:T(8,128)(2,1)S(1)}, u32[]{:S(2)}, u32[]{:S(2)}) collective-permute-start(bf16[1552,128]{1,0:T(8,128)(2,1)S(1)} %keys.1.own_ref), channel_id=1, source_target_pairs={{0,256},{256,0},{1,257},{257,1},{2,258},{258,2},{3,259},{259,3},{4... | collective-permute-start | bytes 1191944 | tf_op jit(solution)/shard_map/ppermute | solution.py:375
  27.4 2.4 %all-gather = bf16[3104,128]{1,0:T(8,128)(2,1)S(1)} all-gather(bf16[1552,128]{1,0:T(8,128)(2,1)S(1)} %keys.1.own_ref), channel_id=2, replica_groups=mesh['yh'=2,'z'=16,'c'=2,'head'=8] {'c'}, dimensions={0}, use_global_device_ids=true | all-gather | bytes 1191936 | tf_op jit(solution)/shard_map/all_gather | solution.py:374
  29.8 10.8 %collective-permute-done = bf16[1552,128]{1,0:T(8,128)(2,1)S(1)} collective-permute-done((bf16[1552,128]{1,0:T(8,128)(2,1)S(1)}, bf16[1552,128]{1,0:T(8,128)(2,1)S(1)}, u32[]{:S(2)}, u32[]{:S(2)}) %collective-permute-start) | collective-permute-done | bytes 397344 | tf_op jit(solution)/shard_map/ppermute | solution.py:375
  40.6 2.4 %all-gather.1 = bf16[3104,128]{1,0:T(8,128)(2,1)S(1)} all-gather(bf16[1552,128]{1,0:T(8,128)(2,1)S(1)} %collective-permute-done), channel_id=3, replica_groups=mesh['yh'=2,'z'=16,'c'=2,'head'=8] {'c'}, dimensions={0}, use_global_device_ids=true | all-gather | bytes 1191936 | tf_op jit(solution)/shard_map/all_gather | solution.py:375
  42.9 14.4 %all-to-all-done.rows_ref = bf16[128,16,128]{2,1,0:T(8,128)(2,1)S(1)} async-done(((bf16[128,16,128]{2,1,0:T(8,128)(2,1)}), bf16[128,16,128]{2,1,0:T(8,128)(2,1)S(1)}, u32[]{:S(2)}, u32[]{:S(2)}) %all-to-all-start) | async-done | bytes 524320 | tf_op jit(solution)/shard_map/all_to_all | solution.py:376
  57.3 0.0 copy-start.4
  57.3 0.0 copy-start.5
  57.3 0.7 copy-done.4
  57.9 0.0 copy-done.5
  58.0 5.7 %first_pass.1 = f32[16,8,256]{2,1,0:T(8,128)} custom-call(s32[16]{0:T(128)S(1)} %copy-done.4, s32[16]{0:T(128)S(1)} %copy-done.5, bf16[128,16,128]{2,1,0:T(8,128)(2,1)S(1)} %all-to-all-done.rows_ref, bf16[2,1552,128]{2,1,0:T(8,128)(2,1)S(1)} %bitcast.5, bf16[2,1552,128]{2,1,0:T(8,128)(2,1)S(1)} %bitcast.7), custom_call_target="tpu_custom_call" | custom-call | tf_op jit(solution)/shard_map/first_pass/pallas_call | solution.py:344
  63.7 1.9 %collective-permute-start.1 = (bf16[128,16,128]{2,1,0:T(8,128)(2,1)S(1)}, bf16[128,16,128]{2,1,0:T(8,128)(2,1)S(1)}, u32[]{:S(2)}, u32[]{:S(2)}) collective-permute-start(bf16[128,16,128]{2,1,0:T(8,128)(2,1)S(1)} %all-to-all-done.rows_ref), channel_id=1, source_target_pairs={{0,8},{8,0},{1,9},{9,1},{2,10},{10,2},{3,11},{11,3},{4,12},{12,4},... | collective-permute-start | bytes 1572872 | tf_op jit(solution)/shard_map/ppermute | solution.py:394
  65.6 3.5 %all-to-all-start.1 = ((f32[16,8,256]{2,1,0:T(8,128)}), f32[16,8,256]{2,1,0:T(8,128)S(1)}, u32[]{:S(2)}, u32[]{:S(2)}) async-start(f32[16,8,256]{2,1,0:T(8,128)} %first_pass.1), calls=%async_computation.1 | async-start | bytes 262144 | tf_op jit(solution)/shard_map/all_to_all | solution.py:397
  69.1 3.1 %collective-permute-start.2 = (bf16[128,16,128]{2,1,0:T(8,128)(2,1)S(1)}, bf16[128,16,128]{2,1,0:T(8,128)(2,1)}, u32[]{:S(2)}, u32[]{:S(2)}) collective-permute-start(bf16[128,16,128]{2,1,0:T(8,128)(2,1)S(1)} %all-to-all-done.rows_ref), channel_id=1, source_target_pairs={{0,256},{256,0},{1,257},{257,1},{2,258},{258,2},{3,259},{259,3},{4... | collective-permute-start | bytes 1572872 | tf_op jit(solution)/shard_map/ppermute | solution.py:395
  72.3 10.7 %all-to-all-done.1.stats_ref = f32[16,8,256]{2,1,0:T(8,128)S(1)} async-done(((f32[16,8,256]{2,1,0:T(8,128)}), f32[16,8,256]{2,1,0:T(8,128)S(1)}, u32[]{:S(2)}, u32[]{:S(2)}) %all-to-all-start.1) | async-done | bytes 131104 | tf_op jit(solution)/shard_map/all_to_all | solution.py:397
  83.0 0.0 collective-permute-done.1.rows_c_ref
  83.0 8.1 %query_pass.1 = (f32[8,256]{1,0:T(8,128)S(1)}, bf16[1024,128]{1,0:T(8,128)(2,1)}) custom-call(s32[16]{0:T(128)S(1)} %copy-done.4, s32[16]{0:T(128)S(1)} %copy-done.5, f32[16,8,256]{2,1,0:T(8,128)S(1)} %all-to-all-done.1.stats_ref, bf16[128,16,128]{2,1,0:T(8,128)(2,1)S(1)} %all-to-all-done.rows_ref, bf16[2,1552,128]{2,1,0:T(8,128)(2,1)S(1)} %bitcast.6, ...), custom_call_target="tpu_custom_call" | custom-call | tf_op jit(solution)/shard_map/query_pass/pallas_call | solution.py:344
  91.0 9.6 %all-to-all-start.2 = ((bf16[128,8,128]{2,1,0:T(8,128)(2,1)}), bf16[128,8,128]{2,1,0:T(8,128)(2,1)S(1)}, u32[]{:S(2)}, u32[]{:S(2)}) async-start(bf16[128,8,128]{2,1,0:T(8,128)(2,1)} %bitcast.2), calls=%async_computation.2 | async-start | bytes 524288 | tf_op jit(solution)/shard_map/all_to_all | solution.py:414
  100.7 0.0 collective-permute-done.2.rows_y_ref
  100.7 1.9 %collective-permute-start.3 = (bf16[128,16,128]{2,1,0:T(8,128)(2,1)}, bf16[128,16,128]{2,1,0:T(8,128)(2,1)S(1)}, u32[]{:S(2)}, u32[]{:S(2)}) collective-permute-start(bf16[128,16,128]{2,1,0:T(8,128)(2,1)} %collective-permute-done.2.rows_y_ref), channel_id=1, source_target_pairs={{0,8},{8,0},{1,9},{9,1},{2,10},{10,2},{3,11},{11,3},{4,12},{12,4},... | collective-permute-start | bytes 1572872 | tf_op jit(solution)/shard_map/ppermute | solution.py:396
  102.6 6.7 %all-gather.2 = f32[32,256]{1,0:T(8,128)S(1)} all-gather(f32[8,256]{1,0:T(8,128)S(1)} %get-tuple-element.19), channel_id=4, replica_groups=mesh['yh'=2,'z'=16,'c'=2,'head'=8] {'yh','c'}, dimensions={0}, use_global_device_ids=true | all-gather | bytes 40960 | tf_op jit(solution)/shard_map/all_gather | solution.py:417
  109.3 0.0 collective-permute-done.3.rows_yc_ref
  109.3 9.7 %key_pass.1 = (bf16[768,128]{1,0:T(8,128)(2,1)}, bf16[768,128]{1,0:T(8,128)(2,1)}, bf16[8,128]{1,0:T(8,128)(2,1)}, bf16[8,128]{1,0:T(8,128)(2,1)}) custom-call(s32[16]{0:T(128)S(1)} %copy-done.4, s32[16]{0:T(128)S(1)} %copy-done.5, f32[4,8,256]{2,1,0:T(8,128)S(1)} %bitcast.10, bf16[128,16,128]{2,1,0:T(8,128)(2,1)S(1)} %all-to-all-done.rows_ref, ...), custom_call_target="tpu_custom_call" | custom-call | tf_op jit(solution)/shard_map/key_pass/pallas_call | solution.py:344
  119.1 2.6 %all-to-all-done.2 = bf16[128,8,128]{2,1,0:T(8,128)(2,1)S(1)} async-done(((bf16[128,8,128]{2,1,0:T(8,128)(2,1)}), bf16[128,8,128]{2,1,0:T(8,128)(2,1)S(1)}, u32[]{:S(2)}, u32[]{:S(2)}) %all-to-all-start.2) | async-done | bytes 262176 | tf_op jit(solution)/shard_map/all_to_all | solution.py:414
  121.7 0.7 finish.1
Async XLA Ops:
  0.6 0.8 copy-start.2
  1.4 0.8 copy-start.3
  3.1 20.6 %copy-start = (bf16[768,128]{1,0:T(8,128)(2,1)S(1)}, bf16[768,128]{1,0:T(8,128)(2,1)}, u32[]{:S(2)}) copy-start(bf16[768,128]{1,0:T(8,128)(2,1)} %k_hbm.1) | copy-start | bytes 589828
  3.1 20.6 %copy-start.1 = (bf16[768,128]{1,0:T(8,128)(2,1)S(1)}, bf16[768,128]{1,0:T(8,128)(2,1)}, u32[]{:S(2)}) copy-start(bf16[768,128]{1,0:T(8,128)(2,1)} %v_hbm.1) | copy-start | bytes 589828
  3.1 20.6 %copy-start.6 = (bf16[8,128]{1,0:T(8,128)(2,1)S(1)}, bf16[8,128]{1,0:T(8,128)(2,1)}, u32[]{:S(2)}) copy-start(bf16[8,128]{1,0:T(8,128)(2,1)} %rk_hbm.1) | copy-start | bytes 6148
  3.2 20.5 %copy-start.7 = (bf16[8,128]{1,0:T(8,128)(2,1)S(1)}, bf16[8,128]{1,0:T(8,128)(2,1)}, u32[]{:S(2)}) copy-start(bf16[8,128]{1,0:T(8,128)(2,1)} %rv_hbm.1) | copy-start | bytes 6148
  3.2 54.1 %all-to-all-start = ((bf16[128,16,128]{2,1,0:T(8,128)(2,1)}), bf16[128,16,128]{2,1,0:T(8,128)(2,1)S(1)}, u32[]{:S(2)}, u32[]{:S(2)}) async-start(bf16[128,16,128]{2,1,0:T(8,128)(2,1)} %send.1), calls=%async_computation | async-start | bytes 1048576 | tf_op jit(solution)/shard_map/all_to_all | solution.py:376
  24.3 16.3 %collective-permute-start = (bf16[1552,128]{1,0:T(8,128)(2,1)S(1)}, bf16[1552,128]{1,0:T(8,128)(2,1)S(1)}, u32[]{:S(2)}, u32[]{:S(2)}) collective-permute-start(bf16[1552,128]{1,0:T(8,128)(2,1)S(1)} %keys.1.own_ref), channel_id=1, source_target_pairs={{0,256},{256,0},{1,257},{257,1},{2,258},{258,2},{3,259},{259,3},{4... | collective-permute-start | bytes 1191944 | tf_op jit(solution)/shard_map/ppermute | solution.py:375
  57.3 0.7 copy-start.4
  57.3 0.7 copy-start.5
  63.7 19.3 %collective-permute-start.1 = (bf16[128,16,128]{2,1,0:T(8,128)(2,1)S(1)}, bf16[128,16,128]{2,1,0:T(8,128)(2,1)S(1)}, u32[]{:S(2)}, u32[]{:S(2)}) collective-permute-start(bf16[128,16,128]{2,1,0:T(8,128)(2,1)S(1)} %all-to-all-done.rows_ref), channel_id=1, source_target_pairs={{0,8},{8,0},{1,9},{9,1},{2,10},{10,2},{3,11},{11,3},{4,12},{12,4},... | collective-permute-start | bytes 1572872 | tf_op jit(solution)/shard_map/ppermute | solution.py:394
  65.6 17.4 %all-to-all-start.1 = ((f32[16,8,256]{2,1,0:T(8,128)}), f32[16,8,256]{2,1,0:T(8,128)S(1)}, u32[]{:S(2)}, u32[]{:S(2)}) async-start(f32[16,8,256]{2,1,0:T(8,128)} %first_pass.1), calls=%async_computation.1 | async-start | bytes 262144 | tf_op jit(solution)/shard_map/all_to_all | solution.py:397
  69.1 31.5 %collective-permute-start.2 = (bf16[128,16,128]{2,1,0:T(8,128)(2,1)S(1)}, bf16[128,16,128]{2,1,0:T(8,128)(2,1)}, u32[]{:S(2)}, u32[]{:S(2)}) collective-permute-start(bf16[128,16,128]{2,1,0:T(8,128)(2,1)S(1)} %all-to-all-done.rows_ref), channel_id=1, source_target_pairs={{0,256},{256,0},{1,257},{257,1},{2,258},{258,2},{3,259},{259,3},{4... | collective-permute-start | bytes 1572872 | tf_op jit(solution)/shard_map/ppermute | solution.py:395
  91.0 30.7 %all-to-all-start.2 = ((bf16[128,8,128]{2,1,0:T(8,128)(2,1)}), bf16[128,8,128]{2,1,0:T(8,128)(2,1)S(1)}, u32[]{:S(2)}, u32[]{:S(2)}) async-start(bf16[128,8,128]{2,1,0:T(8,128)(2,1)} %bitcast.2), calls=%async_computation.2 | async-start | bytes 524288 | tf_op jit(solution)/shard_map/all_to_all | solution.py:414
  100.7 8.6 %collective-permute-start.3 = (bf16[128,16,128]{2,1,0:T(8,128)(2,1)}, bf16[128,16,128]{2,1,0:T(8,128)(2,1)S(1)}, u32[]{:S(2)}, u32[]{:S(2)}) collective-permute-start(bf16[128,16,128]{2,1,0:T(8,128)(2,1)} %collective-permute-done.2.rows_y_ref), channel_id=1, source_target_pairs={{0,8},{8,0},{1,9},{9,1},{2,10},{10,2},{3,11},{11,3},{4,12},{12,4},... | collective-permute-start | bytes 1572872 | tf_op jit(solution)/shard_map/ppermute | solution.py:396

commit v3 on v2

--- a/solution.py
+++ b/solution.py
@@ -1,3 +1,4 @@
+import functools
 import math
 
 import jax
@@ -21,11 +22,13 @@
 CHUNK = 256
 CHUNKS = CLASS // CHUNK
 PROMPT_DEV = 768
-KEYS = 384
-OWN_KEYS = 256
+KEYS1 = 256
+KEYS2 = 768
 WIDE = 2
 SCALE = 1.0 / math.sqrt(HD)
 SCALE2 = SCALE * math.log2(math.e)
+ROW_FLOPS = 5 * 10**9
+KEY_FLOPS = 40 * 10**9
 F32 = jnp.float32
 BF16 = jnp.bfloat16
 
@@ -137,9 +140,9 @@
     return jnp.concatenate([ref[i : i + 1] for i in range(first, first + count)], axis=1)
 
 
-def key_parts(near_ref, far_ref):
+def key_parts(near_ref, far_ref, step):
     return [
-        (ref, c, b) for ref in (near_ref, far_ref) for c in range(2) for b in range(0, PROMPT_DEV, KEYS)
+        (ref, c, b) for ref in (near_ref, far_ref) for c in range(2) for b in range(0, PROMPT_DEV, step)
     ]
 
 
@@ -179,9 +182,9 @@
         place = pl.ds(pl.multiple_of(i * CHUNK, CHUNK), CHUNK)
         q, g = q_ref[place], g_ref[place]
         top, total, inner = (near_ref[n, pl.ds(i, 1)] for n in range(3))
-        for ref, k, b in key_parts(near_kv_ref, far_kv_ref):
-            logits = nt(ref[k, b : b + KEYS], q) * SCALE2
-            dprob = nt(ref[k, PROMPT_DEV + b : PROMPT_DEV + b + KEYS], g)
+        for ref, k, b in key_parts(near_kv_ref, far_kv_ref, KEYS1):
+            logits = nt(ref[k, b : b + KEYS1], q) * SCALE2
+            dprob = nt(ref[k, PROMPT_DEV + b : PROMPT_DEV + b + KEYS1], g)
             now = jnp.maximum(top, jnp.max(logits, axis=0, keepdims=True))
             weights = jnp.exp2(logits - now)
             factor = jnp.exp2(top - now)
@@ -220,8 +223,8 @@
     total = jnp.sum(weights, axis=0)
     mix_ref[:CHUNKS] = top + jnp.log2(total)
     mix_ref[CHUNKS:] = jnp.sum(weights * stats_ref[:, CHUNKS:], axis=0) / total
-    for n, (ref, k, b) in enumerate(key_parts(near_kv_ref, far_kv_ref)):
-        keyt_ref[n] = ref[k, b : b + KEYS].T
+    for n, (ref, k, b) in enumerate(key_parts(near_kv_ref, far_kv_ref, KEYS2)):
+        keyt_ref[n] = ref[k, b : b + KEYS2].T
     chunks = pack_rows(
         lengths_ref, order_ref, rows_ref, yh, c, True, 0, q_ref, g_ref, info_ref
     )
@@ -237,9 +240,9 @@
         q, g = q_ref[place], g_ref[place]
         log, delta = mix_ref[pl.ds(i, 1)], mix_ref[pl.ds(CHUNKS + i, 1)]
         qgrad = jnp.zeros((HD, CHUNK), F32)
-        for n, (ref, k, b) in enumerate(key_parts(near_kv_ref, far_kv_ref)):
-            prob = jnp.exp2(nt(ref[k, b : b + KEYS], q) * SCALE2 - log)
-            dprob = nt(ref[k, PROMPT_DEV + b : PROMPT_DEV + b + KEYS], g)
+        for n, (ref, k, b) in enumerate(key_parts(near_kv_ref, far_kv_ref, KEYS2)):
+            prob = jnp.exp2(nt(ref[k, b : b + KEYS2], q) * SCALE2 - log)
+            dprob = nt(ref[k, PROMPT_DEV + b : PROMPT_DEV + b + KEYS2], g)
             qgrad = qgrad + nn(keyt_ref[n], (prob * (dprob - delta)).astype(BF16))
         qacc_ref[place] = (qgrad.T + nn(near_ref[place], resp_k)) * SCALE
         return 0
@@ -249,18 +252,14 @@
 
 
 def key_kernel(
+    cross,
     lengths_ref,
     order_ref,
     mix_ref,
     rows_ref,
-    rows_c_ref,
     rows_y_ref,
-    rows_yc_ref,
-    own_ref,
-    kg_ref,
-    vg_ref,
-    rkg_ref,
-    rvg_ref,
+    kv_ref,
+    out_ref,
     q_ref,
     g_ref,
     info_ref,
@@ -270,58 +269,62 @@
     vacc_ref,
 ):
     yh, c, z = lax.axis_index("yh"), lax.axis_index("c"), lax.axis_index("z")
+    its_c = 1 - c if cross else c
     kacc_ref[...] = jnp.zeros_like(kacc_ref)
     vacc_ref[...] = jnp.zeros_like(vacc_ref)
     log_ref[...] = jnp.zeros_like(log_ref)
     delta_ref[...] = jnp.zeros_like(delta_ref)
     chunks = 0
-    for far, cross, ref in (
-        (0, 0, rows_ref),
-        (0, 1, rows_c_ref),
-        (1, 0, rows_y_ref),
-        (1, 1, rows_yc_ref),
-    ):
-        its_yh, its_c = (1 - yh if far else yh), (1 - c if cross else c)
-        its = its_yh * 2 + its_c
+    for far, ref in ((0, rows_ref), (1, rows_y_ref)):
+        its_yh = 1 - yh if far else yh
         for i in range(CHUNKS):
-            log_ref[pl.ds(chunks + i, 1)] = mix_ref[its, i : i + 1]
-            delta_ref[pl.ds(chunks + i, 1)] = mix_ref[its, CHUNKS + i : CHUNKS + i + 1]
+            log_ref[pl.ds(chunks + i, 1)] = mix_ref[its_yh, i : i + 1]
+            delta_ref[pl.ds(chunks + i, 1)] = mix_ref[its_yh, CHUNKS + i : CHUNKS + i + 1]
         chunks = pack_rows(
-            lengths_ref, order_ref, ref, its_yh, its_c, not far, chunks, q_ref, g_ref, info_ref
+            lengths_ref, order_ref, ref, its_yh, c, not far, chunks, q_ref, g_ref, info_ref
         )
         if not far:
             info_ref[pl.ds(pl.multiple_of(chunks * CHUNK, CHUNK), CLASS)] = jnp.full(
                 (CLASS, HD), -SLOT, BF16
             )
-    resp = own_ref[2 * PROMPT_DEV :]
+    resp = kv_ref[its_c, 2 * PROMPT_DEV :]
     none = jnp.zeros((ROWS, HD), F32)
     resp_k = jnp.concatenate([resp[:ROWS].astype(F32), none], axis=0).astype(BF16)
     resp_v = jnp.concatenate([resp[ROWS:].astype(F32), none], axis=0).astype(BF16)
-    keys = jnp.concatenate([key_code(z, c), jnp.full((ROWS, 1), 1 << 20, jnp.int32)], axis=0)
-    seen = seen_of(row_code(info_ref[: 2 * CLASS]), keys)
-    log, delta = lanes_of(log_ref, 0, 2 * CHUNKS), lanes_of(delta_ref, 0, 2 * CHUNKS)
-    q, g = q_ref[: 2 * CLASS], g_ref[: 2 * CLASS]
+    keys = jnp.concatenate([key_code(z, its_c), jnp.full((ROWS, 1), 1 << 20, jnp.int32)], axis=0)
+    seen = seen_of(row_code(info_ref[:CLASS]), keys)
+    log, delta = lanes_of(log_ref, 0, CHUNKS), lanes_of(delta_ref, 0, CHUNKS)
+    q, g = q_ref[:CLASS], g_ref[:CLASS]
     prob = jnp.exp2(jnp.where(seen, nt(resp_k, q) * SCALE2 - log, -1e30))
     dscore = (prob * (nt(resp_v, g) - delta)).astype(BF16)
-    rkg_ref[...] = (nn(dscore, q)[:ROWS] * SCALE).astype(BF16)
-    rvg_ref[...] = nn(prob.astype(BF16), g)[:ROWS].astype(BF16)
+    resp_kg = nn(dscore, q)[:ROWS] * SCALE
+    resp_vg = nn(prob.astype(BF16), g)[:ROWS]
+    out_ref[2 * PROMPT_DEV :] = jnp.concatenate([resp_kg, resp_vg], axis=0).astype(out_ref.dtype)
 
     def step(n, _):
         place = pl.ds(pl.multiple_of(n * WIDE * CHUNK, CHUNK), WIDE * CHUNK)
         q, g = q_ref[place], g_ref[place]
         log = jnp.concatenate([log_ref[pl.ds(WIDE * n + i, 1)] for i in range(WIDE)], axis=1)
         delta = jnp.concatenate([delta_ref[pl.ds(WIDE * n + i, 1)] for i in range(WIDE)], axis=1)
-        for b in range(0, PROMPT_DEV, OWN_KEYS):
-            prob = jnp.exp2(nt(own_ref[b : b + OWN_KEYS], q) * SCALE2 - log)
-            dprob = nt(own_ref[PROMPT_DEV + b : PROMPT_DEV + b + OWN_KEYS], g)
-            dscore = (prob * (dprob - delta)).astype(BF16)
-            kacc_ref[b : b + OWN_KEYS] += nn(dscore, q)
-            vacc_ref[b : b + OWN_KEYS] += nn(prob.astype(BF16), g)
+        prob = jnp.exp2(nt(kv_ref[its_c, :PROMPT_DEV], q) * SCALE2 - log)
+        dprob = nt(kv_ref[its_c, PROMPT_DEV : 2 * PROMPT_DEV], g)
+        dscore = (prob * (dprob - delta)).astype(BF16)
+        kacc_ref[...] += nn(dscore, q)
+        vacc_ref[...] += nn(prob.astype(BF16), g)
         return 0
 
     lax.fori_loop(0, (chunks + WIDE - 1) // WIDE, step, 0)
-    kg_ref[...] = (kacc_ref[...] * SCALE).astype(BF16)
-    vg_ref[...] = vacc_ref[...].astype(BF16)
+    out_ref[:PROMPT_DEV] = (kacc_ref[...] * SCALE).astype(out_ref.dtype)
+    out_ref[PROMPT_DEV : 2 * PROMPT_DEV] = vacc_ref[...].astype(out_ref.dtype)
+
+
+def add_kernel(mine_ref, other_ref, kg_ref, vg_ref, rkg_ref, rvg_ref):
+    resp = 2 * PROMPT_DEV
+    kg_ref[...] = (mine_ref[:PROMPT_DEV] + other_ref[:PROMPT_DEV].astype(F32)).astype(BF16)
+    vg_ref[...] = (mine_ref[PROMPT_DEV:resp] + other_ref[PROMPT_DEV:resp].astype(F32)).astype(BF16)
+    rest = mine_ref[resp:] + other_ref[resp:].astype(F32)
+    rkg_ref[...] = rest[:ROWS].astype(BF16)
+    rvg_ref[...] = rest[ROWS:].astype(BF16)
 
 
 def finish_kernel(terms_ref, out_ref):
@@ -340,7 +343,8 @@
     swap = [(0, 1), (1, 0)]
     shape = jax.ShapeDtypeStruct
 
-    def call(kernel, name, out_shape, ints, arrays, scratch=(), space=vmem):
+    def call(kernel, name, out_shape, ints, arrays, scratch=(), space=vmem, flops=0):
+        cost = pl.CostEstimate(flops=flops, bytes_accessed=0, transcendentals=0) if flops else None
         return pl.pallas_call(
             kernel,
             out_shape=out_shape,
@@ -348,6 +352,7 @@
             out_specs=jax.tree.map(lambda _: vmem, out_shape),
             scratch_shapes=list(scratch),
             compiler_params=params,
+            cost_estimate=cost,
             name=name,
         )(*ints, *arrays)
 
@@ -389,13 +394,11 @@
             packed,
             pltpu.VMEM((3, 2 * CHUNKS, CHUNK), F32),
         ],
+        flops=ROW_FLOPS,
     )
     stats, rows = lax.optimization_barrier((stats, rows))
-    rows_c = lax.ppermute(rows, "c", swap)
     rows_y = lax.ppermute(rows, "yh", swap)
-    rows_yc = lax.ppermute(rows_y, "c", swap)
     stats = lax.all_to_all(stats, "z", 0, 0, tiled=True)
-    stats, rows_c = lax.optimization_barrier((stats, rows_c))
     mix, qg = call(
         query_kernel,
         "query_pass",
@@ -407,29 +410,43 @@
             packed,
             packed,
             pltpu.VMEM((CLASS, 2 * ROWS), BF16),
-            pltpu.VMEM((4 * PROMPT_DEV // KEYS, HD, KEYS), BF16),
+            pltpu.VMEM((4 * PROMPT_DEV // KEYS2, HD, KEYS2), BF16),
             pltpu.VMEM((CLASS + BLOCK, HD), F32),
         ],
+        flops=ROW_FLOPS,
     )
     terms = lax.all_to_all(
         qg.reshape(NZ * KVH, GROUP, HD), ("z", "head"), 0, 0, tiled=True
     )
-    mixes = lax.all_gather(mix, ("yh", "c"))
+    mix, rows_y = lax.optimization_barrier((mix, rows_y))
+    mixes = lax.all_gather(mix, "yh")
     acc = pltpu.VMEM((PROMPT_DEV, HD), F32)
-    everyone = pltpu.VMEM((4 * CLASS + BLOCK + 2 * CHUNK, HD), BF16)
-    per_chunk = pltpu.VMEM((6 * CHUNKS, CHUNK), F32)
+    both = pltpu.VMEM((2 * CLASS + BLOCK + 2 * CHUNK, HD), BF16)
+    per_chunk = pltpu.VMEM((4 * CHUNKS, CHUNK), F32)
+
+    def key_pass(cross, name, dtype):
+        return call(
+            functools.partial(key_kernel, cross),
+            name,
+            shape((2 * PROMPT_DEV + 2 * ROWS, HD), dtype),
+            ints,
+            (mixes, rows, rows_y, near_kv),
+            [both, both, both, per_chunk, per_chunk, acc, acc],
+            flops=KEY_FLOPS,
+        )
+
+    other = lax.ppermute(key_pass(1, "other_keys", BF16), "c", swap)
     key_grad, value_grad, resp_key_grad, resp_value_grad = call(
-        key_kernel,
-        "key_pass",
+        add_kernel,
+        "add",
         (
             shape((PROMPT_DEV, HD), BF16),
             shape((PROMPT_DEV, HD), BF16),
             shape((ROWS, HD), BF16),
             shape((ROWS, HD), BF16),
         ),
-        ints,
-        (mixes, rows, rows_c, rows_y, rows_yc, kv),
-        [everyone, everyone, everyone, per_chunk, per_chunk, acc, acc],
+        (),
+        (key_pass(0, "own_keys", F32), other),
     )
     query_grad = call(
         finish_kernel, "finish", shape((1, QH * HD), BF16), (), (terms.reshape(NZ, QH, HD),)

time: 123 us -> 117 us (0.951)
  starting transfers between devices: 43.8 us -> 38.2 us
  waiting for transfers between devices: 38.4 us -> 40.5 us
  Pallas kernels: 25.7 us -> 24.1 us
    all_to_all x1, starting transfers between devices: 9.65 us -> 7.21 us  [shards(): lax.all_to_all(qg.reshape(NZ * KVH, GROUP, HD), ('z', 'head'), 0, 0, tile...]
    ppermute x2 -> x1, starting transfers between devices: 3.83 us -> 1.92 us  [shards(): other = lax.ppermute(key_pass(1, 'other_keys', BF16), 'c', swap)]
    pallas_call x6 -> x8, Pallas kernels: 25.7 us -> 24.1 us  [call(): pl.pallas_call(kernel, out_shape=out_shape, in_specs=[smem] * len(ints) +...]
    all_to_all x1, waiting for transfers between devices: 10.7 us -> 12 us  [shards(): stats = lax.all_to_all(stats, 'z', 0, 0, tiled=True)]
  transfers between devices with their start and end apart: 7 -> 6, of which waited for: 4 -> 4; matrix products, arithmetic and copies ran while one was open for 0% -> 0% of each run, Pallas kernels for 15% -> 14%
where the time goes in v3:
time: 117 us; the launch traced here: 116 us
  waiting for transfers between devices  40.5 us (35%)
  starting transfers between devices  38.2 us (33%)
  Pallas kernels  24.1 us (21%)
  blocking collectives  10.6 us (9%)
  local copies, waits for them, and re-layouts  2.2 us (2%)
    pallas_call x8, Pallas kernels, call(): pl.pallas_call(kernel, out_shape=out_shape, in_specs=[smem] * len(ints) +...  24.1 us
    all_to_all x1, starting transfers between devices, shards(): rows = lax.all_to_all(rows, ('z', 'head'), 0, 0, tiled=True)  20.5 us
    all_to_all x1, waiting for transfers between devices, shards(): rows = lax.all_to_all(rows, ('z', 'head'), 0, 0, tiled=True)  14.4 us
    all_to_all x1, waiting for transfers between devices, shards(): stats = lax.all_to_all(stats, 'z', 0, 0, tiled=True)  12 us
    ppermute x1, waiting for transfers between devices, shards(): far_kv = lax.all_gather(lax.ppermute(kv, 'yh', swap), 'c')  10.8 us
    all_to_all x1, starting transfers between devices, shards(): lax.all_to_all(qg.reshape(NZ * KVH, GROUP, HD), ('z', 'head'), 0, 0, tile...  7.21 us
    all_gather x1, blocking collectives, shards(): mixes = lax.all_gather(mix, 'yh')  5.91 us
    all_to_all x1, starting transfers between devices, shards(): stats = lax.all_to_all(stats, 'z', 0, 0, tiled=True)  3.51 us
  transfers between devices with their start and end apart: 6, of which 4 were waited for; matrix products, arithmetic and copies ran while one was open for 0% of the time, Pallas kernels for 14%

profile of v3, /device:TPU:24, one launch (start us, length us, event | category | flops | bytes accessed | tf_op | source)
XLA Modules:
  0.0 116.4 jit_solution(1608923739585931091)
XLA Ops:
  0.6 0.0 copy-start.2
  0.6 0.7 copy-done.2
  1.4 0.0 copy-start.3
  1.4 0.8 copy-done.3
  2.1 1.0 send.1
  3.1 0.0 copy-start
  3.1 0.0 copy-start.1
  3.2 0.0 copy-start.4
  3.2 0.0 copy-start.5
  3.2 20.5 %all-to-all-start = ((bf16[128,16,128]{2,1,0:T(8,128)(2,1)}), bf16[128,16,128]{2,1,0:T(8,128)(2,1)S(1)}, u32[]{:S(2)}, u32[]{:S(2)}) async-start(bf16[128,16,128]{2,1,0:T(8,128)(2,1)} %send.1), calls=%async_computation | async-start | bytes 1048576 | tf_op jit(solution)/shard_map/all_to_all | solution.py:381
  23.7 0.0 copy-done
  23.7 0.0 copy-done.1
  23.7 0.0 copy-done.4
  23.7 0.0 copy-done.5
  23.7 0.6 keys.1
  24.3 3.1 %collective-permute-start = (bf16[1552,128]{1,0:T(8,128)(2,1)S(1)}, bf16[1552,128]{1,0:T(8,128)(2,1)S(1)}, u32[]{:S(2)}, u32[]{:S(2)}) collective-permute-start(bf16[1552,128]{1,0:T(8,128)(2,1)S(1)} %keys.1), channel_id=1, source_target_pairs={{0,256},{256,0},{1,257},{257,1},{2,258},{258,2},{3,259},{259,3},{4... | collective-permute-start | bytes 1191944 | tf_op jit(solution)/shard_map/ppermute | solution.py:380
  27.4 2.4 %all-gather = bf16[3104,128]{1,0:T(8,128)(2,1)S(1)} all-gather(bf16[1552,128]{1,0:T(8,128)(2,1)S(1)} %keys.1), channel_id=2, replica_groups=mesh['yh'=2,'z'=16,'c'=2,'head'=8] {'c'}, dimensions={0}, use_global_device_ids=true | all-gather | bytes 1191936 | tf_op jit(solution)/shard_map/all_gather | solution.py:379
  29.8 10.8 %collective-permute-done = bf16[1552,128]{1,0:T(8,128)(2,1)S(1)} collective-permute-done((bf16[1552,128]{1,0:T(8,128)(2,1)S(1)}, bf16[1552,128]{1,0:T(8,128)(2,1)S(1)}, u32[]{:S(2)}, u32[]{:S(2)}) %collective-permute-start) | collective-permute-done | bytes 397344 | tf_op jit(solution)/shard_map/ppermute | solution.py:380
  40.6 2.4 %all-gather.1 = bf16[3104,128]{1,0:T(8,128)(2,1)S(1)} all-gather(bf16[1552,128]{1,0:T(8,128)(2,1)S(1)} %collective-permute-done), channel_id=3, replica_groups=mesh['yh'=2,'z'=16,'c'=2,'head'=8] {'c'}, dimensions={0}, use_global_device_ids=true | all-gather | bytes 1191936 | tf_op jit(solution)/shard_map/all_gather | solution.py:380
  42.9 14.4 %all-to-all-done.rows_ref = bf16[128,16,128]{2,1,0:T(8,128)(2,1)S(1)} async-done(((bf16[128,16,128]{2,1,0:T(8,128)(2,1)}), bf16[128,16,128]{2,1,0:T(8,128)(2,1)S(1)}, u32[]{:S(2)}, u32[]{:S(2)}) %all-to-all-start) | async-done | bytes 524320 | tf_op jit(solution)/shard_map/all_to_all | solution.py:381
  57.3 0.0 copy-start.6
  57.3 0.0 copy-start.7
  57.3 0.7 copy-done.6
  57.9 0.0 copy-done.7
  58.0 5.6 %first_pass.1 = f32[16,8,256]{2,1,0:T(8,128)} custom-call(s32[16]{0:T(128)S(1)} %copy-done.6, s32[16]{0:T(128)S(1)} %copy-done.7, bf16[128,16,128]{2,1,0:T(8,128)(2,1)S(1)} %all-to-all-done.rows_ref, bf16[2,1552,128]{2,1,0:T(8,128)(2,1)S(1)} %bitcast.6, bf16[2,1552,128]{2,1,0:T(8,128)(2,1)S(1)} %bitcast.10), custom_call_target="tpu_custom_call" | custom-call | flops 5000000000 | tf_op jit(solution)/shard_map/first_pass/pallas_call | solution.py:348
  63.5 3.5 %all-to-all-start.1 = ((f32[16,8,256]{2,1,0:T(8,128)}), f32[16,8,256]{2,1,0:T(8,128)S(1)}, u32[]{:S(2)}, u32[]{:S(2)}) async-start(f32[16,8,256]{2,1,0:T(8,128)} %first_pass.1), calls=%async_computation.1 | async-start | bytes 262144 | tf_op jit(solution)/shard_map/all_to_all | solution.py:401
  67.1 1.9 %collective-permute-start.1 = (bf16[128,16,128]{2,1,0:T(8,128)(2,1)S(1)}, bf16[128,16,128]{2,1,0:T(8,128)(2,1)S(1)}, u32[]{:S(2)}, u32[]{:S(2)}) collective-permute-start(bf16[128,16,128]{2,1,0:T(8,128)(2,1)S(1)} %all-to-all-done.rows_ref), channel_id=1, source_target_pairs={{0,256},{256,0},{1,257},{257,1},{2,258},{258,2},{3,259},{259,3},{4... | collective-permute-start | bytes 1572872 | tf_op jit(solution)/shard_map/ppermute | solution.py:400
  69.0 12.0 %all-to-all-done.1.stats_ref = f32[16,8,256]{2,1,0:T(8,128)S(1)} async-done(((f32[16,8,256]{2,1,0:T(8,128)}), f32[16,8,256]{2,1,0:T(8,128)S(1)}, u32[]{:S(2)}, u32[]{:S(2)}) %all-to-all-start.1) | async-done | bytes 131104 | tf_op jit(solution)/shard_map/all_to_all | solution.py:401
  81.0 6.3 %query_pass.1 = (f32[8,256]{1,0:T(8,128)S(1)}, bf16[1024,128]{1,0:T(8,128)(2,1)}) custom-call(s32[16]{0:T(128)S(1)} %copy-done.6, s32[16]{0:T(128)S(1)} %copy-done.7, f32[16,8,256]{2,1,0:T(8,128)S(1)} %all-to-all-done.1.stats_ref, bf16[128,16,128]{2,1,0:T(8,128)(2,1)S(1)} %all-to-all-done.rows_ref, bf16[2,1552,128]{2,1,0:T(8,128)(2,1)S(1)} %bitcast.7, ...), custom_call_target="tpu_custom_call" | custom-call | flops 5000000000 | tf_op jit(solution)/shard_map/query_pass/pallas_call | solution.py:348
  87.3 7.2 %all-to-all-start.2 = ((bf16[128,8,128]{2,1,0:T(8,128)(2,1)}), bf16[128,8,128]{2,1,0:T(8,128)(2,1)S(1)}, u32[]{:S(2)}, u32[]{:S(2)}) async-start(bf16[128,8,128]{2,1,0:T(8,128)(2,1)} %bitcast.2), calls=%async_computation.2 | async-start | bytes 524288 | tf_op jit(solution)/shard_map/all_to_all | solution.py:418
  94.5 0.0 collective-permute-done.1.rows_y_ref
  94.6 5.9 %all-gather.2 = f32[16,256]{1,0:T(8,128)S(1)} all-gather(f32[8,256]{1,0:T(8,128)S(1)} %get-tuple-element.19), channel_id=4, replica_groups=mesh['yh'=2,'z'=16,'c'=2,'head'=8] {'yh'}, dimensions={0}, use_global_device_ids=true | all-gather | bytes 24576 | tf_op jit(solution)/shard_map/all_gather | solution.py:422
  100.5 4.6 %other_keys.1 = bf16[1552,128]{1,0:T(8,128)(2,1)S(1)} custom-call(s32[16]{0:T(128)S(1)} %copy-done.6, s32[16]{0:T(128)S(1)} %copy-done.7, f32[2,8,256]{2,1,0:T(8,128)S(1)} %bitcast.12, bf16[128,16,128]{2,1,0:T(8,128)(2,1)S(1)} %all-to-all-done.rows_ref, bf16[128,16,128]{2,1,0:T(8,128)(2,1)S(1)} %collective-permute-done.1.rows_y_ref, ...), custom_call_target="tpu_custom_call" | custom-call | flops 40000000000 | tf_op jit(solution)/shard_map/other_keys/pallas_call | solution.py:348
  105.0 1.9 %collective-permute-start.2 = (bf16[1552,128]{1,0:T(8,128)(2,1)S(1)}, bf16[1552,128]{1,0:T(8,128)(2,1)S(1)}, u32[]{:S(2)}, u32[]{:S(2)}) collective-permute-start(bf16[1552,128]{1,0:T(8,128)(2,1)S(1)} %other_keys.1), channel_id=1, source_target_pairs={{0,8},{8,0},{1,9},{9,1},{2,10},{10,2},{3,11},{11,3},{4,12},{12,4},... | collective-permute-start | bytes 1191944 | tf_op jit(solution)/shard_map/ppermute | solution.py:438
  107.0 4.6 %own_keys.1.mine_ref = f32[1552,128]{1,0:T(8,128)S(1)} custom-call(s32[16]{0:T(128)S(1)} %copy-done.6, s32[16]{0:T(128)S(1)} %copy-done.7, f32[2,8,256]{2,1,0:T(8,128)S(1)} %bitcast.13, bf16[128,16,128]{2,1,0:T(8,128)(2,1)S(1)} %all-to-all-done.rows_ref, bf16[128,16,128]{2,1,0:T(8,128)(2,1)S(1)} %collective-permute-done.1.rows_y_ref, ...), custom_call_target="tpu_custom_call" | custom-call | flops 40000000000 | tf_op jit(solution)/shard_map/own_keys/pallas_call | solution.py:348
  111.6 0.0 collective-permute-done.2.other_ref
  111.6 0.8 add.1
  112.4 3.4 %all-to-all-done.2 = bf16[128,8,128]{2,1,0:T(8,128)(2,1)S(1)} async-done(((bf16[128,8,128]{2,1,0:T(8,128)(2,1)}), bf16[128,8,128]{2,1,0:T(8,128)(2,1)S(1)}, u32[]{:S(2)}, u32[]{:S(2)}) %all-to-all-start.2) | async-done | bytes 262176 | tf_op jit(solution)/shard_map/all_to_all | solution.py:418
  115.8 0.7 finish.1
Async XLA Ops:
  0.6 0.8 copy-start.2
  1.4 0.8 copy-start.3
  3.1 20.6 %copy-start = (bf16[768,128]{1,0:T(8,128)(2,1)S(1)}, bf16[768,128]{1,0:T(8,128)(2,1)}, u32[]{:S(2)}) copy-start(bf16[768,128]{1,0:T(8,128)(2,1)} %k_hbm.1) | copy-start | bytes 589828
  3.1 20.6 %copy-start.1 = (bf16[768,128]{1,0:T(8,128)(2,1)S(1)}, bf16[768,128]{1,0:T(8,128)(2,1)}, u32[]{:S(2)}) copy-start(bf16[768,128]{1,0:T(8,128)(2,1)} %v_hbm.1) | copy-start | bytes 589828
  3.2 20.5 %copy-start.4 = (bf16[8,128]{1,0:T(8,128)(2,1)S(1)}, bf16[8,128]{1,0:T(8,128)(2,1)}, u32[]{:S(2)}) copy-start(bf16[8,128]{1,0:T(8,128)(2,1)} %rk_hbm.1) | copy-start | bytes 6148
  3.2 20.5 %copy-start.5 = (bf16[8,128]{1,0:T(8,128)(2,1)S(1)}, bf16[8,128]{1,0:T(8,128)(2,1)}, u32[]{:S(2)}) copy-start(bf16[8,128]{1,0:T(8,128)(2,1)} %rv_hbm.1) | copy-start | bytes 6148
  3.2 54.1 %all-to-all-start = ((bf16[128,16,128]{2,1,0:T(8,128)(2,1)}), bf16[128,16,128]{2,1,0:T(8,128)(2,1)S(1)}, u32[]{:S(2)}, u32[]{:S(2)}) async-start(bf16[128,16,128]{2,1,0:T(8,128)(2,1)} %send.1), calls=%async_computation | async-start | bytes 1048576 | tf_op jit(solution)/shard_map/all_to_all | solution.py:381
  24.3 16.3 %collective-permute-start = (bf16[1552,128]{1,0:T(8,128)(2,1)S(1)}, bf16[1552,128]{1,0:T(8,128)(2,1)S(1)}, u32[]{:S(2)}, u32[]{:S(2)}) collective-permute-start(bf16[1552,128]{1,0:T(8,128)(2,1)S(1)} %keys.1), channel_id=1, source_target_pairs={{0,256},{256,0},{1,257},{257,1},{2,258},{258,2},{3,259},{259,3},{4... | collective-permute-start | bytes 1191944 | tf_op jit(solution)/shard_map/ppermute | solution.py:380
  57.3 0.7 copy-start.6
  57.3 0.7 copy-start.7
  63.5 17.5 %all-to-all-start.1 = ((f32[16,8,256]{2,1,0:T(8,128)}), f32[16,8,256]{2,1,0:T(8,128)S(1)}, u32[]{:S(2)}, u32[]{:S(2)}) async-start(f32[16,8,256]{2,1,0:T(8,128)} %first_pass.1), calls=%async_computation.1 | async-start | bytes 262144 | tf_op jit(solution)/shard_map/all_to_all | solution.py:401
  67.1 27.5 %collective-permute-start.1 = (bf16[128,16,128]{2,1,0:T(8,128)(2,1)S(1)}, bf16[128,16,128]{2,1,0:T(8,128)(2,1)S(1)}, u32[]{:S(2)}, u32[]{:S(2)}) collective-permute-start(bf16[128,16,128]{2,1,0:T(8,128)(2,1)S(1)} %all-to-all-done.rows_ref), channel_id=1, source_target_pairs={{0,256},{256,0},{1,257},{257,1},{2,258},{258,2},{3,259},{259,3},{4... | collective-permute-start | bytes 1572872 | tf_op jit(solution)/shard_map/ppermute | solution.py:400
  87.3 28.4 %all-to-all-start.2 = ((bf16[128,8,128]{2,1,0:T(8,128)(2,1)}), bf16[128,8,128]{2,1,0:T(8,128)(2,1)S(1)}, u32[]{:S(2)}, u32[]{:S(2)}) async-start(bf16[128,8,128]{2,1,0:T(8,128)(2,1)} %bitcast.2), calls=%async_computation.2 | async-start | bytes 524288 | tf_op jit(solution)/shard_map/all_to_all | solution.py:418
  105.0 6.5 %collective-permute-start.2 = (bf16[1552,128]{1,0:T(8,128)(2,1)S(1)}, bf16[1552,128]{1,0:T(8,128)(2,1)S(1)}, u32[]{:S(2)}, u32[]{:S(2)}) collective-permute-start(bf16[1552,128]{1,0:T(8,128)(2,1)S(1)} %other_keys.1), channel_id=1, source_target_pairs={{0,8},{8,0},{1,9},{9,1},{2,10},{10,2},{3,11},{11,3},{4,12},{12,4},... | collective-permute-start | bytes 1191944 | tf_op jit(solution)/shard_map/ppermute | solution.py:438

commit v4 on v3

--- a/solution.py
+++ b/solution.py
@@ -41,38 +41,43 @@
     return jnp.dot(a, b, preferred_element_type=F32)
 
 
-def live_rows(lengths_ref, order_ref, yh, c, z):
-    length = lengths_ref[order_ref[yh * (NRESP // 2) + z // 2]]
+def live_rows(lens_ref, yh, c, z):
+    length = lens_ref[yh * (NRESP // 2) + z // 2]
     return jnp.clip(length - ((z % 2) * 2 + c) * ROWS, 0, ROWS)
 
 
-def pack_rows(lengths_ref, order_ref, rows_ref, yh, c, near, start, q_ref, g_ref, info_ref):
+def chunks_of(lens_ref, yh, c):
+    pairs = 0
+    for z in range(NZ):
+        pairs = pairs + (live_rows(lens_ref, yh, c, z) + 1) // 2
+    return (pairs * 16 + CHUNK - 1) // CHUNK
+
+
+def pack_rows(lens_ref, rows_ref, yh, c, q_ref, g_ref, info_ref):
     in_block = lax.broadcasted_iota(jnp.int32, (BLOCK, HD), 0)
-    at = start * (CHUNK // 16)
+    at = 0
     for z in range(NZ):
-        live = live_rows(lengths_ref, order_ref, yh, c, z)
+        live = live_rows(lens_ref, yh, c, z)
         place = pl.ds(pl.multiple_of(at * 16, 16), BLOCK)
         both = rows_ref[z * ROWS : (z + 1) * ROWS].astype(F32)
         q_ref[place] = both[:, :GROUP].reshape(BLOCK, HD).astype(BF16)
         g = both[:, GROUP:].reshape(BLOCK, HD)
         g_ref[place] = jnp.where(in_block < live * GROUP, g, 0.0).astype(BF16)
-        if near:
-            code = (z // 2) * SLOT + ((z % 2) * 2 + c) * ROWS + in_block // GROUP
-            info_ref[place] = code.astype(F32).astype(BF16)
+        code = (z // 2) * SLOT + ((z % 2) * 2 + c) * ROWS + in_block // GROUP
+        info_ref[place] = code.astype(F32).astype(BF16)
         at = at + (live + 1) // 2
-    rest = pl.ds(pl.multiple_of(at * 16, 16), 2 * CHUNK)
-    q_ref[rest] = jnp.zeros((2 * CHUNK, HD), BF16)
-    g_ref[rest] = jnp.zeros((2 * CHUNK, HD), BF16)
-    if near:
-        info_ref[rest] = jnp.full((2 * CHUNK, HD), -SLOT, BF16)
+    rest = pl.ds(pl.multiple_of(at * 16, 16), CLASS)
+    q_ref[rest] = jnp.zeros((CLASS, HD), BF16)
+    g_ref[rest] = jnp.zeros((CLASS, HD), BF16)
+    info_ref[rest] = jnp.full((CLASS, HD), -SLOT, BF16)
     return (at * 16 + CHUNK - 1) // CHUNK
 
 
-def unpack_rows(lengths_ref, order_ref, yh, c, acc_ref, out_ref):
+def unpack_rows(lens_ref, yh, c, acc_ref, out_ref):
     in_block = lax.broadcasted_iota(jnp.int32, (BLOCK, HD), 0)
     at = 0
     for z in range(NZ):
-        live = live_rows(lengths_ref, order_ref, yh, c, z)
+        live = live_rows(lens_ref, yh, c, z)
         block = acc_ref[pl.ds(pl.multiple_of(at * 16, 16), BLOCK)]
         out_ref[z * BLOCK : (z + 1) * BLOCK] = jnp.where(
             in_block < live * GROUP, block, 0.0
@@ -115,7 +120,9 @@
         rows_ref[z * KVH : (z + 1) * KVH] = hold_ref[...].astype(BF16)
 
 
-def keys_kernel(k_hbm, v_hbm, rk_hbm, rv_hbm, kv_ref, rk_ref, rv_ref, sems):
+def keys_kernel(
+    lengths_ref, order_ref, k_hbm, v_hbm, rk_hbm, rv_hbm, kv_ref, lens_ref, rk_ref, rv_ref, sems
+):
     copies = [
         pltpu.make_async_copy(k_hbm, kv_ref.at[:PROMPT_DEV], sems.at[0]),
         pltpu.make_async_copy(v_hbm, kv_ref.at[PROMPT_DEV : 2 * PROMPT_DEV], sems.at[1]),
@@ -127,6 +134,8 @@
     for copy in copies:
         copy.wait()
     kv_ref[2 * PROMPT_DEV :] = stack8(rk_ref[...], rv_ref[...])
+    for slot in range(NRESP):
+        lens_ref[slot] = lengths_ref[order_ref[slot]]
 
 
 def resp_of(kv_ref):
@@ -147,12 +156,13 @@
 
 
 def first_kernel(
-    lengths_ref,
-    order_ref,
+    lens_ref,
     rows_ref,
     near_kv_ref,
     far_kv_ref,
     out_ref,
+    packed_ref,
+    code_ref,
     stat_ref,
     q_ref,
     g_ref,
@@ -160,13 +170,16 @@
     near_ref,
 ):
     yh, c, z = lax.axis_index("yh"), lax.axis_index("c"), lax.axis_index("z")
-    chunks = pack_rows(
-        lengths_ref, order_ref, rows_ref, yh, c, True, 0, q_ref, g_ref, info_ref
-    )
+    chunks = pack_rows(lens_ref, rows_ref, yh, c, q_ref, g_ref, info_ref)
+    packed_ref[0] = q_ref[:CLASS]
+    packed_ref[1] = g_ref[:CLASS]
     stat_ref[...] = jnp.zeros_like(stat_ref)
     resp_k, resp_v = resp_of(near_kv_ref)
     keys = jnp.concatenate([key_code(z, 0), key_code(z, 1)], axis=0)
-    seen = seen_of(row_code(info_ref[:CLASS]), keys)
+    codes = row_code(info_ref[:CLASS])
+    for i in range(CHUNKS):
+        code_ref[i : i + 1] = codes[:, i * CHUNK : (i + 1) * CHUNK]
+    seen = seen_of(codes, keys)
     logits = jnp.where(seen, nt(resp_k, q_ref[:CLASS]) * SCALE2, -1e30)
     top = jnp.maximum(jnp.max(logits, axis=0, keepdims=True), -1e29)
     weights = jnp.exp2(logits - top)
@@ -201,19 +214,16 @@
 
 
 def query_kernel(
-    lengths_ref,
-    order_ref,
+    lens_ref,
     stats_ref,
-    rows_ref,
+    packed_ref,
+    code_ref,
     near_kv_ref,
     far_kv_ref,
+    keyt_ref,
     mix_ref,
     qg_ref,
-    q_ref,
-    g_ref,
-    info_ref,
     near_ref,
-    keyt_ref,
     qacc_ref,
 ):
     yh, c, z = lax.axis_index("yh"), lax.axis_index("c"), lax.axis_index("z")
@@ -223,46 +233,46 @@
     total = jnp.sum(weights, axis=0)
     mix_ref[:CHUNKS] = top + jnp.log2(total)
     mix_ref[CHUNKS:] = jnp.sum(weights * stats_ref[:, CHUNKS:], axis=0) / total
-    for n, (ref, k, b) in enumerate(key_parts(near_kv_ref, far_kv_ref, KEYS2)):
-        keyt_ref[n] = ref[k, b : b + KEYS2].T
-    chunks = pack_rows(
-        lengths_ref, order_ref, rows_ref, yh, c, True, 0, q_ref, g_ref, info_ref
-    )
+    chunks = chunks_of(lens_ref, yh, c)
     resp_k, resp_v = resp_of(near_kv_ref)
     keys = jnp.concatenate([key_code(z, 0), key_code(z, 1)], axis=0)
-    seen = seen_of(row_code(info_ref[:CLASS]), keys)
+    seen = seen_of(lanes_of(code_ref, 0, CHUNKS), keys)
     log, delta = lanes_of(mix_ref, 0, CHUNKS), lanes_of(mix_ref, CHUNKS, CHUNKS)
-    prob = jnp.exp2(jnp.where(seen, nt(resp_k, q_ref[:CLASS]) * SCALE2 - log, -1e30))
-    near_ref[...] = (prob * (nt(resp_v, g_ref[:CLASS]) - delta)).astype(BF16).T
+    prob = jnp.exp2(jnp.where(seen, nt(resp_k, packed_ref[0]) * SCALE2 - log, -1e30))
+    near_ref[...] = (prob * (nt(resp_v, packed_ref[1]) - delta)).astype(BF16).T
 
     def chunk(i, _):
         place = pl.ds(pl.multiple_of(i * CHUNK, CHUNK), CHUNK)
-        q, g = q_ref[place], g_ref[place]
+        q, g = packed_ref[0, place], packed_ref[1, place]
         log, delta = mix_ref[pl.ds(i, 1)], mix_ref[pl.ds(CHUNKS + i, 1)]
         qgrad = jnp.zeros((HD, CHUNK), F32)
-        for n, (ref, k, b) in enumerate(key_parts(near_kv_ref, far_kv_ref, KEYS2)):
-            prob = jnp.exp2(nt(ref[k, b : b + KEYS2], q) * SCALE2 - log)
-            dprob = nt(ref[k, PROMPT_DEV + b : PROMPT_DEV + b + KEYS2], g)
+        for n, (ref, core, b) in enumerate(key_parts(near_kv_ref, far_kv_ref, KEYS2)):
+            prob = jnp.exp2(nt(ref[core, b : b + KEYS2], q) * SCALE2 - log)
+            dprob = nt(ref[core, PROMPT_DEV + b : PROMPT_DEV + b + KEYS2], g)
             qgrad = qgrad + nn(keyt_ref[n], (prob * (dprob - delta)).astype(BF16))
         qacc_ref[place] = (qgrad.T + nn(near_ref[place], resp_k)) * SCALE
         return 0
 
     lax.fori_loop(0, chunks, chunk, 0)
-    unpack_rows(lengths_ref, order_ref, yh, c, qacc_ref, qg_ref)
+    unpack_rows(lens_ref, yh, c, qacc_ref, qg_ref)
+
+
+def turn_kernel(near_kv_ref, far_kv_ref, keyt_ref):
+    for n, (ref, core, b) in enumerate(key_parts(near_kv_ref, far_kv_ref, KEYS2)):
+        keyt_ref[n] = ref[core, b : b + KEYS2].T
 
 
 def key_kernel(
     cross,
-    lengths_ref,
-    order_ref,
+    lens_ref,
     mix_ref,
-    rows_ref,
-    rows_y_ref,
+    near_ref,
+    far_ref,
+    code_ref,
     kv_ref,
     out_ref,
     q_ref,
     g_ref,
-    info_ref,
     log_ref,
     delta_ref,
     kacc_ref,
@@ -275,26 +285,23 @@
     log_ref[...] = jnp.zeros_like(log_ref)
     delta_ref[...] = jnp.zeros_like(delta_ref)
     chunks = 0
-    for far, ref in ((0, rows_ref), (1, rows_y_ref)):
-        its_yh = 1 - yh if far else yh
+    for its_yh, ref in ((yh, near_ref), (1 - yh, far_ref)):
         for i in range(CHUNKS):
             log_ref[pl.ds(chunks + i, 1)] = mix_ref[its_yh, i : i + 1]
             delta_ref[pl.ds(chunks + i, 1)] = mix_ref[its_yh, CHUNKS + i : CHUNKS + i + 1]
-        chunks = pack_rows(
-            lengths_ref, order_ref, ref, its_yh, c, not far, chunks, q_ref, g_ref, info_ref
-        )
-        if not far:
-            info_ref[pl.ds(pl.multiple_of(chunks * CHUNK, CHUNK), CLASS)] = jnp.full(
-                (CLASS, HD), -SLOT, BF16
-            )
+        place = pl.ds(pl.multiple_of(chunks * CHUNK, CHUNK), CLASS)
+        q_ref[place], g_ref[place] = ref[0], ref[1]
+        chunks = chunks + chunks_of(lens_ref, its_yh, c)
+    after = pl.ds(pl.multiple_of(chunks * CHUNK, CHUNK), CHUNK)
+    q_ref[after] = g_ref[after] = jnp.zeros((CHUNK, HD), BF16)
     resp = kv_ref[its_c, 2 * PROMPT_DEV :]
     none = jnp.zeros((ROWS, HD), F32)
     resp_k = jnp.concatenate([resp[:ROWS].astype(F32), none], axis=0).astype(BF16)
     resp_v = jnp.concatenate([resp[ROWS:].astype(F32), none], axis=0).astype(BF16)
     keys = jnp.concatenate([key_code(z, its_c), jnp.full((ROWS, 1), 1 << 20, jnp.int32)], axis=0)
-    seen = seen_of(row_code(info_ref[:CLASS]), keys)
-    log, delta = lanes_of(log_ref, 0, CHUNKS), lanes_of(delta_ref, 0, CHUNKS)
-    q, g = q_ref[:CLASS], g_ref[:CLASS]
+    seen = seen_of(lanes_of(code_ref, 0, CHUNKS), keys)
+    log, delta = lanes_of(mix_ref.at[yh], 0, CHUNKS), lanes_of(mix_ref.at[yh], CHUNKS, CHUNKS)
+    q, g = near_ref[0], near_ref[1]
     prob = jnp.exp2(jnp.where(seen, nt(resp_k, q) * SCALE2 - log, -1e30))
     dscore = (prob * (nt(resp_v, g) - delta)).astype(BF16)
     resp_kg = nn(dscore, q)[:ROWS] * SCALE
@@ -318,7 +325,12 @@
     out_ref[PROMPT_DEV : 2 * PROMPT_DEV] = vacc_ref[...].astype(out_ref.dtype)
 
 
-def add_kernel(mine_ref, other_ref, kg_ref, vg_ref, rkg_ref, rvg_ref):
+def finish_kernel(
+    terms_ref, mine_ref, other_ref, qg_ref, kg_ref, vg_ref, rkg_ref, rvg_ref
+):
+    total = jnp.sum(terms_ref[...].astype(F32), axis=0)
+    for h in range(QH):
+        qg_ref[:, h * HD : (h + 1) * HD] = total[h : h + 1].astype(BF16)
     resp = 2 * PROMPT_DEV
     kg_ref[...] = (mine_ref[:PROMPT_DEV] + other_ref[:PROMPT_DEV].astype(F32)).astype(BF16)
     vg_ref[...] = (mine_ref[PROMPT_DEV:resp] + other_ref[PROMPT_DEV:resp].astype(F32)).astype(BF16)
@@ -327,31 +339,26 @@
     rvg_ref[...] = rest[ROWS:].astype(BF16)
 
 
-def finish_kernel(terms_ref, out_ref):
-    total = jnp.sum(terms_ref[...].astype(F32), axis=0)
-    for h in range(QH):
-        out_ref[:, h * HD : (h + 1) * HD] = total[h : h + 1].astype(BF16)
-
-
 def shards(
     queries, out_grad, resp_keys, resp_values, prompt_keys, prompt_values, resp_lengths, resp_order
 ):
     vmem = pl.BlockSpec(memory_space=pltpu.VMEM)
     smem = pl.BlockSpec(memory_space=pltpu.SMEM)
     hbm = pl.BlockSpec(memory_space=pltpu.HBM)
-    params = pltpu.CompilerParams(vmem_limit_bytes=32 * 1024 * 1024)
     swap = [(0, 1), (1, 0)]
     shape = jax.ShapeDtypeStruct
 
-    def call(kernel, name, out_shape, ints, arrays, scratch=(), space=vmem, flops=0):
+    def call(
+        kernel, name, out_shape, ints, arrays, scratch=(), space=vmem, flops=0, out=None, limit=32
+    ):
         cost = pl.CostEstimate(flops=flops, bytes_accessed=0, transcendentals=0) if flops else None
         return pl.pallas_call(
             kernel,
             out_shape=out_shape,
             in_specs=[smem] * len(ints) + [space] * len(arrays),
-            out_specs=jax.tree.map(lambda _: vmem, out_shape),
+            out_specs=out or jax.tree.map(lambda _: vmem, out_shape),
             scratch_shapes=list(scratch),
-            compiler_params=params,
+            compiler_params=pltpu.CompilerParams(vmem_limit_bytes=limit * 1024 * 1024),
             cost_estimate=cost,
             name=name,
         )(*ints, *arrays)
@@ -365,63 +372,69 @@
         (queries, out_grad),
         [whole, whole, pltpu.VMEM((KVH, 2 * GROUP, HD), F32), pltpu.SemaphoreType.DMA((2,))],
         hbm,
+        limit=60,
     )
     few = pltpu.VMEM((ROWS, HD), BF16)
-    kv = call(
+    kv, lens = call(
         keys_kernel,
         "keys",
-        shape((2 * PROMPT_DEV + 2 * ROWS, HD), BF16),
-        (),
+        (shape((2 * PROMPT_DEV + 2 * ROWS, HD), BF16), shape((NRESP,), jnp.int32)),
+        (resp_lengths, resp_order),
         (prompt_keys, prompt_values, resp_keys, resp_values),
         [few, few, pltpu.SemaphoreType.DMA((4,))],
         hbm,
+        out=(vmem, smem),
     )
     near_kv = lax.all_gather(kv, "c")
     far_kv = lax.all_gather(lax.ppermute(kv, "yh", swap), "c")
     rows = lax.all_to_all(rows, ("z", "head"), 0, 0, tiled=True)
-    packed = pltpu.VMEM((CLASS + BLOCK + 2 * CHUNK, HD), BF16)
-    ints = (resp_lengths, resp_order)
-    stats = call(
+    keyt = call(
+        turn_kernel,
+        "turn",
+        shape((4 * PROMPT_DEV // KEYS2, HD, KEYS2), BF16),
+        (),
+        (near_kv, far_kv),
+    )
+    hold = pltpu.VMEM((2 * CLASS + BLOCK, HD), BF16)
+    ints = (lens,)
+    lanes = shape((2 * CHUNKS, CHUNK), F32)
+    stats, packed, code = call(
         first_kernel,
         "first_pass",
-        shape((NZ, 2 * CHUNKS, CHUNK), F32),
+        (
+            shape((NZ, 2 * CHUNKS, CHUNK), F32),
+            shape((2, CLASS, HD), BF16),
+            shape((2 * CHUNKS, CHUNK), jnp.int32),
+        ),
         ints,
         (rows, near_kv, far_kv),
         [
             pltpu.VMEM((2 * CHUNKS, CHUNK), F32),
-            packed,
-            packed,
-            packed,
+            hold,
+            hold,
+            hold,
             pltpu.VMEM((3, 2 * CHUNKS, CHUNK), F32),
         ],
         flops=ROW_FLOPS,
     )
-    stats, rows = lax.optimization_barrier((stats, rows))
-    rows_y = lax.ppermute(rows, "yh", swap)
+    far_packed = lax.ppermute(packed, "yh", swap)
     stats = lax.all_to_all(stats, "z", 0, 0, tiled=True)
     mix, qg = call(
         query_kernel,
         "query_pass",
-        (shape((2 * CHUNKS, CHUNK), F32), shape((CLASS, HD), BF16)),
+        (lanes, shape((CLASS, HD), BF16)),
         ints,
-        (stats, rows, near_kv, far_kv),
-        [
-            packed,
-            packed,
-            packed,
-            pltpu.VMEM((CLASS, 2 * ROWS), BF16),
-            pltpu.VMEM((4 * PROMPT_DEV // KEYS2, HD, KEYS2), BF16),
-            pltpu.VMEM((CLASS + BLOCK, HD), F32),
-        ],
+        (stats, packed, code, near_kv, far_kv, keyt),
+        [pltpu.VMEM((CLASS, 2 * ROWS), BF16), pltpu.VMEM((CLASS + BLOCK, HD), F32)],
         flops=ROW_FLOPS,
     )
     terms = lax.all_to_all(
         qg.reshape(NZ * KVH, GROUP, HD), ("z", "head"), 0, 0, tiled=True
     )
-    mix, rows_y = lax.optimization_barrier((mix, rows_y))
+    mix, far_packed = lax.optimization_barrier((mix, far_packed))
     mixes = lax.all_gather(mix, "yh")
     acc = pltpu.VMEM((PROMPT_DEV, HD), F32)
-    both = pltpu.VMEM((2 * CLASS + BLOCK + 2 * CHUNK, HD), BF16)
+    both = pltpu.VMEM((2 * CLASS + CHUNK, HD), BF16)
     per_chunk = pltpu.VMEM((4 * CHUNKS, CHUNK), F32)
 
     def key_pass(cross, name, dtype):
@@ -430,28 +443,25 @@
             name,
             shape((2 * PROMPT_DEV + 2 * ROWS, HD), dtype),
             ints,
-            (mixes, rows, rows_y, near_kv),
-            [both, both, both, per_chunk, per_chunk, acc, acc],
+            (mixes, packed, far_packed, code, near_kv),
+            [both, both, per_chunk, per_chunk, acc, acc],
             flops=KEY_FLOPS,
         )
 
     other = lax.ppermute(key_pass(1, "other_keys", BF16), "c", swap)
-    key_grad, value_grad, resp_key_grad, resp_value_grad = call(
-        add_kernel,
-        "add",
+    return call(
+        finish_kernel,
+        "finish",
         (
+            shape((1, QH * HD), BF16),
             shape((PROMPT_DEV, HD), BF16),
             shape((PROMPT_DEV, HD), BF16),
             shape((ROWS, HD), BF16),
             shape((ROWS, HD), BF16),
         ),
         (),
-        (key_pass(0, "own_keys", F32), other),
-    )
-    query_grad = call(
-        finish_kernel, "finish", shape((1, QH * HD), BF16), (), (terms.reshape(NZ, QH, HD),)
-    )
-    return query_grad, key_grad, value_grad, resp_key_grad, resp_value_grad
+        (terms.reshape(NZ, QH, HD), key_pass(0, "own_keys", F32), other),
+    )
 
 
 def solution(mesh):

time: 117 us -> 113 us (0.966)
  waiting for transfers between devices: 40.5 us -> 34.9 us
  local copies, waits for them, and re-layouts: 2.2 us -> 0.04 us
  starting transfers between devices: 38.2 us -> 40.2 us
  Pallas kernels: 24.1 us -> 25.7 us
    all_to_all x1, waiting for transfers between devices: 12 us -> 9.74 us  [shards(): stats = lax.all_to_all(stats, 'z', 0, 0, tiled=True)]
    all_to_all x1, waiting for transfers between devices: 3.38 us -> 1.17 us  [shards(): lax.all_to_all(qg.reshape(NZ * KVH, GROUP, HD), ('z', 'head'), 0, 0, tile...]
    unnamed x16 -> x12, local copies, waits for them, and re-layouts: 2.2 us -> 0.04 us
    pallas_call x8, Pallas kernels: 24.1 us -> 25.7 us  [call(): pl.pallas_call(kernel, out_shape=out_shape, in_specs=[smem] * len(ints) +...]
    all_to_all x1, waiting for transfers between devices: 14.4 us -> 13 us  [shards(): rows = lax.all_to_all(rows, ('z', 'head'), 0, 0, tiled=True)]
    ppermute x1, starting transfers between devices: 1.92 us -> 3.14 us  [shards(): far_packed = lax.ppermute(packed, 'yh', swap)]
  transfers between devices with their start and end apart: 6 -> 6, of which waited for: 4 -> 4; matrix products, arithmetic and copies ran while one was open for 0% -> 0% of each run, Pallas kernels for 14% -> 16%
where the time goes in v4:
time: 113 us; the launch traced here: 112 us
  starting transfers between devices  40.2 us (36%)
  waiting for transfers between devices  34.9 us (31%)
  Pallas kernels  25.7 us (23%)
  blocking collectives  10.6 us (9%)
    pallas_call x8, Pallas kernels, call(): pl.pallas_call(kernel, out_shape=out_shape, in_specs=[smem] * len(ints) +...  25.7 us
    all_to_all x1, starting transfers between devices, shards(): rows = lax.all_to_all(rows, ('z', 'head'), 0, 0, tiled=True)  20.5 us
    all_to_all x1, waiting for transfers between devices, shards(): rows = lax.all_to_all(rows, ('z', 'head'), 0, 0, tiled=True)  13 us
    ppermute x1, waiting for transfers between devices, shards(): far_kv = lax.all_gather(lax.ppermute(kv, 'yh', swap), 'c')  11 us
    all_to_all x1, waiting for transfers between devices, shards(): stats = lax.all_to_all(stats, 'z', 0, 0, tiled=True)  9.74 us
    all_to_all x1, starting transfers between devices, shards(): lax.all_to_all(qg.reshape(NZ * KVH, GROUP, HD), ('z', 'head'), 0, 0, tile...  8 us
    all_gather x1, blocking collectives, shards(): mixes = lax.all_gather(mix, 'yh')  5.87 us
    all_to_all x1, starting transfers between devices, shards(): stats = lax.all_to_all(stats, 'z', 0, 0, tiled=True)  3.51 us
  transfers between devices with their start and end apart: 6, of which 4 were waited for; matrix products, arithmetic and copies ran while one was open for 0% of the time, Pallas kernels for 16%

profile of v4, /device:TPU:24, one launch (start us, length us, event | category | flops | bytes accessed | tf_op | source)
XLA Modules:
  0.0 112.2 jit_solution(10557330328888269321)
XLA Ops:
  0.6 1.7 %send.1 = bf16[128,16,128]{2,1,0:T(8,128)(2,1)} custom-call(bf16[1,8192]{1,0:T(2,128)(2,1)} %q_hbm.1, bf16[1,8192]{1,0:T(2,128)(2,1)} %g_hbm.1), custom_call_target="tpu_custom_call" | custom-call | tf_op jit(solution)/shard_map/send/pallas_call | solution.py:355
  2.3 0.0 copy-start
  2.3 0.0 copy-start.1
  2.3 0.0 copy-start.2
  2.3 0.0 copy-start.3
  2.4 0.0 copy-start.4
  2.4 0.0 copy-start.5
  2.4 20.5 %all-to-all-start = ((bf16[128,16,128]{2,1,0:T(8,128)(2,1)}), bf16[128,16,128]{2,1,0:T(8,128)(2,1)S(1)}, u32[]{:S(2)}, u32[]{:S(2)}) async-start(bf16[128,16,128]{2,1,0:T(8,128)(2,1)} %send.1), calls=%async_computation | async-start | bytes 1048576 | tf_op jit(solution)/shard_map/all_to_all | solution.py:390
  22.9 0.0 copy-done
  22.9 0.0 copy-done.1
  22.9 0.0 copy-done.2
  22.9 0.0 copy-done.3
  22.9 0.0 copy-done.4
  22.9 0.0 copy-done.5
  22.9 1.7 %keys.1 = (bf16[1552,128]{1,0:T(8,128)(2,1)S(1)}, s32[16]{0:T(128)S(1)}) custom-call(s32[16]{0:T(128)S(1)} %copy-done.4, s32[16]{0:T(128)S(1)} %copy-done.5, bf16[768,128]{1,0:T(8,128)(2,1)S(1)} %copy-done, bf16[768,128]{1,0:T(8,128)(2,1)S(1)} %copy-done.1, bf16[8,128]{1,0:T(8,128)(2,1)S(1)} %copy-done.2, bf16[8,128]{1,0:T(8,128)(2,1)S(1)} %copy-done.3), custom_call_target="tpu_custom_call" | custom-call | tf_op jit(solution)/shard_map/keys/pallas_call | solution.py:355
  24.7 3.1 %collective-permute-start = (bf16[1552,128]{1,0:T(8,128)(2,1)S(1)}, bf16[1552,128]{1,0:T(8,128)(2,1)S(1)}, u32[]{:S(2)}, u32[]{:S(2)}) collective-permute-start(bf16[1552,128]{1,0:T(8,128)(2,1)S(1)} %get-tuple-element.15), channel_id=1, source_target_pairs={{0,256},{256,0},{1,257},{257,1},{2,258},{258,2},{3,259},{259,3},{4... | collective-permute-start | bytes 1191944 | tf_op jit(solution)/shard_map/ppermute | solution.py:389
  27.8 2.4 %all-gather = bf16[3104,128]{1,0:T(8,128)(2,1)S(1)} all-gather(bf16[1552,128]{1,0:T(8,128)(2,1)S(1)} %get-tuple-element.15), channel_id=2, replica_groups=mesh['yh'=2,'z'=16,'c'=2,'head'=8] {'c'}, dimensions={0}, use_global_device_ids=true | all-gather | bytes 1191936 | tf_op jit(solution)/shard_map/all_gather | solution.py:388
  30.2 11.0 %collective-permute-done = bf16[1552,128]{1,0:T(8,128)(2,1)S(1)} collective-permute-done((bf16[1552,128]{1,0:T(8,128)(2,1)S(1)}, bf16[1552,128]{1,0:T(8,128)(2,1)S(1)}, u32[]{:S(2)}, u32[]{:S(2)}) %collective-permute-start) | collective-permute-done | bytes 397344 | tf_op jit(solution)/shard_map/ppermute | solution.py:389
  41.2 2.4 %all-gather.1 = bf16[3104,128]{1,0:T(8,128)(2,1)S(1)} all-gather(bf16[1552,128]{1,0:T(8,128)(2,1)S(1)} %collective-permute-done), channel_id=3, replica_groups=mesh['yh'=2,'z'=16,'c'=2,'head'=8] {'c'}, dimensions={0}, use_global_device_ids=true | all-gather | bytes 1191936 | tf_op jit(solution)/shard_map/all_gather | solution.py:389
  43.5 13.0 %all-to-all-done.rows_ref = bf16[128,16,128]{2,1,0:T(8,128)(2,1)S(1)} async-done(((bf16[128,16,128]{2,1,0:T(8,128)(2,1)}), bf16[128,16,128]{2,1,0:T(8,128)(2,1)S(1)}, u32[]{:S(2)}, u32[]{:S(2)}) %all-to-all-start) | async-done | bytes 524320 | tf_op jit(solution)/shard_map/all_to_all | solution.py:390
  56.5 5.7 %first_pass.1 = (f32[16,8,256]{2,1,0:T(8,128)}, bf16[2,1024,128]{2,1,0:T(8,128)(2,1)S(1)}, s32[8,256]{1,0:T(8,128)S(1)}) custom-call(s32[16]{0:T(128)S(1)} %get-tuple-element.14.lens_ref, bf16[128,16,128]{2,1,0:T(8,128)(2,1)S(1)} %all-to-all-done.rows_ref, bf16[2,1552,128]{2,1,0:T(8,128)(2,1)S(1)} %bitcast.5, bf16[2,1552,128]{2,1,0:T(8,128)(2,1)S(1)} %bitcast.10), custom_call_target="tpu_custom_call" | custom-call | flops 5000000000 | tf_op jit(solution)/shard_map/first_pass/pallas_call | solution.py:355
  62.2 3.5 %all-to-all-start.1 = ((f32[16,8,256]{2,1,0:T(8,128)}), f32[16,8,256]{2,1,0:T(8,128)S(1)}, u32[]{:S(2)}, u32[]{:S(2)}) async-start(f32[16,8,256]{2,1,0:T(8,128)} %get-tuple-element.16), calls=%async_computation.1 | async-start | bytes 262144 | tf_op jit(solution)/shard_map/all_to_all | solution.py:421
  65.7 3.1 %collective-permute-start.1 = (bf16[2,1024,128]{2,1,0:T(8,128)(2,1)S(1)}, bf16[2,1024,128]{2,1,0:T(8,128)(2,1)}, u32[]{:S(2)}, u32[]{:S(2)}) collective-permute-start(bf16[2,1024,128]{2,1,0:T(8,128)(2,1)S(1)} %get-tuple-element.17.packed_ref.near_ref), channel_id=1, source_target_pairs={{0,256},{256,0},{1,257},{257,1},{2,258},{258,2},{3,259},{259,3},{4... | collective-permute-start | bytes 1572872 | tf_op jit(solution)/shard_map/ppermute | solution.py:420
  68.9 0.3 turn.1.keyt_ref
  69.2 9.7 %all-to-all-done.1.stats_ref = f32[16,8,256]{2,1,0:T(8,128)S(1)} async-done(((f32[16,8,256]{2,1,0:T(8,128)}), f32[16,8,256]{2,1,0:T(8,128)S(1)}, u32[]{:S(2)}, u32[]{:S(2)}) %all-to-all-start.1) | async-done | bytes 131104 | tf_op jit(solution)/shard_map/all_to_all | solution.py:421
  78.9 6.1 %query_pass.1 = (f32[8,256]{1,0:T(8,128)S(1)}, bf16[1024,128]{1,0:T(8,128)(2,1)}) custom-call(s32[16]{0:T(128)S(1)} %get-tuple-element.14.lens_ref, f32[16,8,256]{2,1,0:T(8,128)S(1)} %all-to-all-done.1.stats_ref, bf16[2,1024,128]{2,1,0:T(8,128)(2,1)S(1)} %get-tuple-element.17.packed_ref.near_ref, s32[8,256]{1,0:T(8,128)S(1)} %get-tuple-element.18.code_ref, ...), custom_call_target="tpu_custom_call" | custom-call | flops 5000000000 | tf_op jit(solution)/shard_map/query_pass/pallas_call | solution.py:355
  84.9 8.0 %all-to-all-start.2 = ((bf16[128,8,128]{2,1,0:T(8,128)(2,1)}), bf16[128,8,128]{2,1,0:T(8,128)(2,1)S(1)}, u32[]{:S(2)}, u32[]{:S(2)}) async-start(bf16[128,8,128]{2,1,0:T(8,128)(2,1)} %bitcast.2), calls=%async_computation.2 | async-start | bytes 524288 | tf_op jit(solution)/shard_map/all_to_all | solution.py:431
  93.0 0.0 collective-permute-done.1.far_ref
  93.0 5.9 %all-gather.2 = f32[16,256]{1,0:T(8,128)S(1)} all-gather(f32[8,256]{1,0:T(8,128)S(1)} %get-tuple-element.21), channel_id=4, replica_groups=mesh['yh'=2,'z'=16,'c'=2,'head'=8] {'yh'}, dimensions={0}, use_global_device_ids=true | all-gather | bytes 24576 | tf_op jit(solution)/shard_map/all_gather | solution.py:435
  98.8 4.7 %other_keys.1 = bf16[1552,128]{1,0:T(8,128)(2,1)S(1)} custom-call(s32[16]{0:T(128)S(1)} %get-tuple-element.14.lens_ref, f32[2,8,256]{2,1,0:T(8,128)S(1)} %bitcast.14, bf16[2,1024,128]{2,1,0:T(8,128)(2,1)S(1)} %get-tuple-element.17.packed_ref.near_ref, bf16[2,1024,128]{2,1,0:T(8,128)(2,1)} %collective-permute-done.1.far_ref, ...), custom_call_target="tpu_custom_call" | custom-call | flops 40000000000 | tf_op jit(solution)/shard_map/other_keys/pallas_call | solution.py:355
  103.6 1.9 %collective-permute-start.2 = (bf16[1552,128]{1,0:T(8,128)(2,1)S(1)}, bf16[1552,128]{1,0:T(8,128)(2,1)S(1)}, u32[]{:S(2)}, u32[]{:S(2)}) collective-permute-start(bf16[1552,128]{1,0:T(8,128)(2,1)S(1)} %other_keys.1), channel_id=1, source_target_pairs={{0,8},{8,0},{1,9},{9,1},{2,10},{10,2},{3,11},{11,3},{4,12},{12,4},... | collective-permute-start | bytes 1191944 | tf_op jit(solution)/shard_map/ppermute | solution.py:451
  105.5 4.7 %own_keys.1.mine_ref = f32[1552,128]{1,0:T(8,128)S(1)} custom-call(s32[16]{0:T(128)S(1)} %get-tuple-element.14.lens_ref, f32[2,8,256]{2,1,0:T(8,128)S(1)} %bitcast.15, bf16[2,1024,128]{2,1,0:T(8,128)(2,1)S(1)} %get-tuple-element.17.packed_ref.near_ref, bf16[2,1024,128]{2,1,0:T(8,128)(2,1)} %collective-permute-done.1.far_ref, ...), custom_call_target="tpu_custom_call" | custom-call | flops 40000000000 | tf_op jit(solution)/shard_map/own_keys/pallas_call | solution.py:355
  110.2 0.0 collective-permute-done.2.other_ref
  110.2 1.2 %all-to-all-done.2 = bf16[128,8,128]{2,1,0:T(8,128)(2,1)S(1)} async-done(((bf16[128,8,128]{2,1,0:T(8,128)(2,1)}), bf16[128,8,128]{2,1,0:T(8,128)(2,1)S(1)}, u32[]{:S(2)}, u32[]{:S(2)}) %all-to-all-start.2) | async-done | bytes 262176 | tf_op jit(solution)/shard_map/all_to_all | solution.py:431
  111.4 0.8 finish.1
Async XLA Ops:
  2.3 20.6 %copy-start = (bf16[768,128]{1,0:T(8,128)(2,1)S(1)}, bf16[768,128]{1,0:T(8,128)(2,1)}, u32[]{:S(2)}) copy-start(bf16[768,128]{1,0:T(8,128)(2,1)} %k_hbm.1) | copy-start | bytes 589828
  2.3 20.6 %copy-start.1 = (bf16[768,128]{1,0:T(8,128)(2,1)S(1)}, bf16[768,128]{1,0:T(8,128)(2,1)}, u32[]{:S(2)}) copy-start(bf16[768,128]{1,0:T(8,128)(2,1)} %v_hbm.1) | copy-start | bytes 589828
  2.3 20.6 %copy-start.2 = (bf16[8,128]{1,0:T(8,128)(2,1)S(1)}, bf16[8,128]{1,0:T(8,128)(2,1)}, u32[]{:S(2)}) copy-start(bf16[8,128]{1,0:T(8,128)(2,1)} %rk_hbm.1) | copy-start | bytes 6148
  2.3 20.6 %copy-start.3 = (bf16[8,128]{1,0:T(8,128)(2,1)S(1)}, bf16[8,128]{1,0:T(8,128)(2,1)}, u32[]{:S(2)}) copy-start(bf16[8,128]{1,0:T(8,128)(2,1)} %rv_hbm.1) | copy-start | bytes 6148
  2.4 20.6 %copy-start.4 = (s32[16]{0:T(128)S(1)}, s32[16]{0:T(128)}, u32[]{:S(2)}) copy-start(s32[16]{0:T(128)} %lengths_ref.1) | copy-start | bytes 196
  2.4 20.6 %copy-start.5 = (s32[16]{0:T(128)S(1)}, s32[16]{0:T(128)}, u32[]{:S(2)}) copy-start(s32[16]{0:T(128)} %order_ref.1) | copy-start | bytes 196
  2.4 54.1 %all-to-all-start = ((bf16[128,16,128]{2,1,0:T(8,128)(2,1)}), bf16[128,16,128]{2,1,0:T(8,128)(2,1)S(1)}, u32[]{:S(2)}, u32[]{:S(2)}) async-start(bf16[128,16,128]{2,1,0:T(8,128)(2,1)} %send.1), calls=%async_computation | async-start | bytes 1048576 | tf_op jit(solution)/shard_map/all_to_all | solution.py:390
  24.7 16.5 %collective-permute-start = (bf16[1552,128]{1,0:T(8,128)(2,1)S(1)}, bf16[1552,128]{1,0:T(8,128)(2,1)S(1)}, u32[]{:S(2)}, u32[]{:S(2)}) collective-permute-start(bf16[1552,128]{1,0:T(8,128)(2,1)S(1)} %get-tuple-element.15), channel_id=1, source_target_pairs={{0,256},{256,0},{1,257},{257,1},{2,258},{258,2},{3,259},{259,3},{4... | collective-permute-start | bytes 1191944 | tf_op jit(solution)/shard_map/ppermute | solution.py:389
  62.2 16.7 %all-to-all-start.1 = ((f32[16,8,256]{2,1,0:T(8,128)}), f32[16,8,256]{2,1,0:T(8,128)S(1)}, u32[]{:S(2)}, u32[]{:S(2)}) async-start(f32[16,8,256]{2,1,0:T(8,128)} %get-tuple-element.16), calls=%async_computation.1 | async-start | bytes 262144 | tf_op jit(solution)/shard_map/all_to_all | solution.py:421
  65.7 27.2 %collective-permute-start.1 = (bf16[2,1024,128]{2,1,0:T(8,128)(2,1)S(1)}, bf16[2,1024,128]{2,1,0:T(8,128)(2,1)}, u32[]{:S(2)}, u32[]{:S(2)}) collective-permute-start(bf16[2,1024,128]{2,1,0:T(8,128)(2,1)S(1)} %get-tuple-element.17.packed_ref.near_ref), channel_id=1, source_target_pairs={{0,256},{256,0},{1,257},{257,1},{2,258},{258,2},{3,259},{259,3},{4... | collective-permute-start | bytes 1572872 | tf_op jit(solution)/shard_map/ppermute | solution.py:420
  84.9 26.4 %all-to-all-start.2 = ((bf16[128,8,128]{2,1,0:T(8,128)(2,1)}), bf16[128,8,128]{2,1,0:T(8,128)(2,1)S(1)}, u32[]{:S(2)}, u32[]{:S(2)}) async-start(bf16[128,8,128]{2,1,0:T(8,128)(2,1)} %bitcast.2), calls=%async_computation.2 | async-start | bytes 524288 | tf_op jit(solution)/shard_map/all_to_all | solution.py:431
  103.6 6.7 %collective-permute-start.2 = (bf16[1552,128]{1,0:T(8,128)(2,1)S(1)}, bf16[1552,128]{1,0:T(8,128)(2,1)S(1)}, u32[]{:S(2)}, u32[]{:S(2)}) collective-permute-start(bf16[1552,128]{1,0:T(8,128)(2,1)S(1)} %other_keys.1), channel_id=1, source_target_pairs={{0,8},{8,0},{1,9},{9,1},{2,10},{10,2},{3,11},{11,3},{4,12},{12,4},... | collective-permute-start | bytes 1191944 | tf_op jit(solution)/shard_map/ppermute | solution.py:451
